TPU v7x, 32 devices: a whole 2x2x4 slice. The times are simulated.
32 devices in a mesh: groups: 2 (over x), chan: 16 (over z, y, core).
Axes of the slice: x: 2, y: 2, z: 4, core: 2. Of those that a mesh axis runs over, the one named last changes fastest.
Arguments:
- sky_data: bfloat16 [1024, 512, 2, 256], P('groups', 'chan'), parts along dimension 0, may hold values from -1.1953125 to 1.1953125
- beam_gains: bfloat16 [1024, 512, 256], P('groups', 'chan'), parts along dimension 0, may hold values from 0.099609375 to 1
- mixing: float32 [1024, 4], P(('groups', 'chan')), parts along dimension 0, may hold values from -0.25 to 0.25
- noise_levels: int32 [512], P('chan'), may hold values from 1 to 16
- threshold_levels: int32 [4, 2], replicated, may hold values from 1 to 8
- start_sources: float32 [1024, 4, 256], P(('groups', 'chan')), parts along dimension 0, may hold values from -6 to 6
Outputs:
- sources: float32 [1024, 4, 256], P(('groups', 'chan')), parts along dimension 0
There are 2 independent parts, one for each index of `groups`. A program takes and returns all parts, laid end to end along the dimension named above; an argument that names none is the same for every part. Nothing has to cross between parts.
All inputs are finite; a program needn't handle non-finite values.
Results may differ from a plain program's by a relative error of at most 0.025.
Values may be sent and summed in bfloat16 or wider, within the bound.
A program may use at most 128 MiB of HBM per device.

v0:
```python
import math

import jax
import jax.numpy as jnp
from jax import lax
from jax.sharding import PartitionSpec as P

ITERS = 2


def padded_2(cells, sides, width):
    for axis, dim in sides:
        count = lax.axis_size(axis)
        ends = count - 1
        head = lax.slice_in_dim(cells, 0, width, axis=dim)
        tail = lax.slice_in_dim(cells, cells.shape[dim] - width, cells.shape[dim], axis=dim)
        cells = jnp.concatenate(
            [
                lax.ppermute(tail, axis, [(i, (i + 1) % count) for i in range(ends)]),
                cells,
                lax.ppermute(head, axis, [((i + 1) % count, i) for i in range(ends)]),
            ],
            axis=dim,
        )
    return cells


def dft_tables(length):
    positions = jnp.arange(length, dtype=jnp.int32)
    angles = (positions[:, None] * positions[None, :] % length).astype(jnp.float32) * (
        2.0 * math.pi / length
    )
    norm_factor = 1.0 / math.sqrt(length)
    return (
        (jnp.cos(angles) * norm_factor).astype(jnp.bfloat16),
        (-jnp.sin(angles) * norm_factor).astype(jnp.bfloat16),
    )


def column_part(rounded, col_cat):
    row_count, source_count, col_count = rounded.shape
    product = jnp.dot(
        rounded.reshape(row_count * source_count, col_count),
        col_cat,
        preferred_element_type=jnp.float32,
    )
    return product.astype(jnp.bfloat16).reshape(row_count, source_count * 2 * col_count)


def combine_forward(real_prod, imag_prod, source_count, col_count):
    real_prod = real_prod.reshape(real_prod.shape[0], source_count, 2, col_count)
    imag_prod = imag_prod.reshape(imag_prod.shape[0], source_count, 2, col_count)
    real_out = real_prod[:, :, 0] - imag_prod[:, :, 1]
    imag_out = real_prod[:, :, 1] + imag_prod[:, :, 0]
    return jnp.stack([real_out, imag_out], axis=2)


def inverse_rows(row_real, row_imag, packed_grad, col_back, source_count, col_count):
    real_prod = jnp.dot(row_real, packed_grad, preferred_element_type=jnp.float32)
    imag_prod = jnp.dot(row_imag, packed_grad, preferred_element_type=jnp.float32)
    real_prod = real_prod.reshape(real_prod.shape[0], source_count, 2, col_count)
    imag_prod = imag_prod.reshape(imag_prod.shape[0], source_count, 2, col_count)
    real_out = real_prod[:, :, 0] + imag_prod[:, :, 1]
    imag_out = real_prod[:, :, 1] - imag_prod[:, :, 0]
    joined = jnp.concatenate([real_out, imag_out], axis=-1).astype(jnp.bfloat16)
    result = jnp.dot(
        joined.reshape(-1, 2 * col_count), col_back, preferred_element_type=jnp.float32
    )
    return result.reshape(real_prod.shape[0], source_count, col_count)


def block_gradient(fourier, data_block, beam_block, mix_block, level_block):
    predicted = jnp.einsum("ct,ktzl->kczl", mix_block, fourier)
    beam_gain = beam_block.astype(jnp.float32)[:, :, None, :]
    residual = data_block.astype(jnp.float32) - beam_gain * predicted
    weight = level_block.astype(jnp.float32) * 0.25
    weighted = weight[None, :, None, None] * beam_gain * residual
    summed = jnp.einsum("cs,kczl->kszl", mix_block, weighted)
    return summed.astype(jnp.bfloat16)


def smooth_rows(padded, spacing, row_count):
    return (
        padded[0:row_count]
        + 2.0 * padded[spacing : spacing + row_count]
        + padded[2 * spacing : 2 * spacing + row_count]
    ) * 0.25


def smooth_cols(values, spacing):
    padded = jnp.pad(values, ((0, 0), (0, 0), (spacing, spacing)))
    return (
        padded[..., : -2 * spacing]
        + 2.0 * padded[..., spacing:-spacing]
        + padded[..., 2 * spacing :]
    ) * 0.25


def shrink(values, bound_value):
    return values - jnp.clip(values, -bound_value, bound_value)


def combine_scales(updated, smooth_one, coarse, fine_bound, coarse_bound):
    return (
        coarse
        + shrink(smooth_one - coarse, coarse_bound)
        + shrink(updated - smooth_one, fine_bound)
    )


def body(sky_data, beam_gains, mixing, noise_levels, threshold_levels, start_sources):
    strip_rows, source_count, col_count = start_sources.shape
    full_rows = strip_rows * lax.axis_size("chan")
    row_real, row_imag = dft_tables(full_rows)
    col_real, col_imag = dft_tables(col_count)
    col_cat = jnp.concatenate([col_real, col_imag], axis=1)
    col_back = jnp.concatenate([col_real, col_imag], axis=0)
    bounds = threshold_levels.astype(jnp.float32) * 0.05
    fine_bound = bounds[:, 0][:, None]
    coarse_bound = bounds[:, 1][:, None]
    sources = start_sources
    for iteration in range(ITERS):
        rounded = sources.astype(jnp.bfloat16)
        gathered = lax.all_gather(rounded, "chan", axis=0, tiled=True)
        packed = column_part(gathered, col_cat)
        fourier = combine_forward(
            jnp.dot(row_real, packed, preferred_element_type=jnp.float32),
            jnp.dot(row_imag, packed, preferred_element_type=jnp.float32),
            source_count,
            col_count,
        )
        grad_local = block_gradient(fourier, sky_data, beam_gains, mixing, noise_levels)
        packed_grad = grad_local.reshape(full_rows, source_count * 2 * col_count)
        gradient = lax.psum_scatter(
            inverse_rows(row_real, row_imag, packed_grad, col_back, source_count, col_count),
            "chan",
            scatter_dimension=0,
            tiled=True,
        )
        updated = sources + gradient
        fine_pad = padded_2(updated, (("chan", 0),), 1)
        smooth_one = smooth_cols(smooth_rows(fine_pad, 1, strip_rows), 1)
        coarse_pad = padded_2(smooth_one, (("chan", 0),), 2)
        coarse = smooth_cols(smooth_rows(coarse_pad, 2, strip_rows), 2)
        sources = combine_scales(updated, smooth_one, coarse, fine_bound, coarse_bound)
    return sources


def solution(mesh):
    return jax.shard_map(
        body,
        mesh=mesh,
        in_specs=(
            P("groups", "chan", None, None),
            P("groups", "chan", None),
            P(("groups", "chan"), None),
            P("chan"),
            P(),
            P(("groups", "chan"), None, None),
        ),
        out_specs=P(("groups", "chan"), None, None),
        check_vma=False,
    )
```

profile of v0, /device:TPU:1, one launch (start us, length us, event | category | flops | bytes accessed | tf_op | source)
XLA Modules:
  0.0 385.0 jit_solution(10828506220403828621)
XLA Ops:
  8.2 11.3 %convert_element_type.111 = f32[512,32,256]{2,1,0:T(8,128)} convert(bf16[512,32,256]{2,1,0:T(8,128)(2,1)} %param.7) | non-fusion elementwise | flops 4194304 | bytes 25165824 | tf_op jit(solution)/shard_map/convert_element_type | solution.py:74
  20.6 11.7 %broadcast_multiply_fusion = f32[512,32,256]{2,1,0:T(8,128)} fusion(f32[32]{0:T(128)S(1)} %convert_multiply_fusion.1, bf16[512,32,256]{2,1,0:T(8,128)(2,1)} %param.7), kind=kLoop, calls=%fused_computation.16 | loop fusion | flops 8388608 | bytes 25165952 | tf_op jit(solution)/shard_map/mul | solution.py:77
  32.3 17.7 %all-gather.3.cloned.1.call-done = bf16[512,4,256]{2,1,0:T(4,128)(2,1)} async-done(((bf16[32,4,256]{2,1,0:T(4,128)(2,1)}), bf16[512,4,256]{2,1,0:T(4,128)(2,1)}) %all-gather.3.cloned.1.call-update) | async-done | bytes 1048592 | tf_op jit(solution)/shard_map/all_gather | solution.py:124
  54.7 3.1 reshape.71
  60.5 6.6 %fusion.67 = f32[512,4,2,256]{3,0,2,1:T(8,128)S(1)} fusion(bf16[4,2,256,512]{3,2,1,0:T(8,128)(2,1)} %bitcast.123), kind=kOutput, calls=%fused_computation.76 | convolution fusion | flops 1078198272 | bytes 6291456 | tf_op jit(solution)/shard_map/dot_general | solution.py:128
  67.2 4.9 %fusion.73 = f32[512,4,2,256]{3,0,2,1:T(8,128)S(1)} fusion(bf16[4,2,256,512]{3,2,1,0:T(8,128)(2,1)S(1)} %bitcast.124), kind=kOutput, calls=%fused_computation.78 | convolution fusion | flops 1077936128 | bytes 6291456 | tf_op jit(solution)/shard_map/dot_general | solution.py:127
  73.7 24.1 %convert_bitcast_fusion.1 = bf16[512,4,2,256]{3,1,2,0:T(4,128)(2,1)} fusion(f32[512,32,256]{2,1,0:T(8,128)} %convert_element_type.111, f32[512,32,256]{2,1,0:T(8,128)} %broadcast_multiply_fusion, bf16[512,32,2,256]{3,2,1,0:T(2,128)(2,1)} %param.6, bf16[512,4,2,256]{3,0,2,1:T(8,128)(2,1)S(1)} %pad_maximum_fusion, f32[32,4]{0,1:T(4,128)S(1)} %copy-done.2), kind=kOutput, calls=%fused_computation.57 | convolution fusion | flops 176160896 | bytes 54526464 | tf_op jit(solution)/shard_map/cs,kczl->kszl/dot_general | solution.py:78
  97.8 3.0 copy.40
  100.7 7.3 %fusion.39 = f32[512,4,2,256]{0,3,2,1:T(8,128)S(1)} fusion(bf16[512,4,2,256]{0,3,2,1:T(8,128)(2,1)S(1)} %copy.40), kind=kOutput, calls=%fused_computation.52 | convolution fusion | flops 1078198272 | bytes 6291456 | tf_op jit(solution)/shard_map/dot_general | solution.py:60
  108.1 7.3 %fusion.41 = f32[512,4,2,256]{0,3,2,1:T(8,128)S(1)} fusion(bf16[512,4,2,256]{0,3,2,1:T(8,128)(2,1)S(1)} %copy.40), kind=kOutput, calls=%fused_computation.54 | convolution fusion | flops 1077936128 | bytes 6291456 | tf_op jit(solution)/shard_map/dot_general | solution.py:59
  118.7 58.6 %reduce-scatter.3.cloned.1.call-done = f32[32,4,256]{2,0,1:T(8,128)} async-done(((f32[512,4,256]{2,0,1:T(8,128)}), f32[32,4,256]{2,0,1:T(8,128)}) %reduce-scatter.3.cloned.1.call-update) | async-done | bytes 131088 | tf_op jit(solution)/shard_map/reduce_scatter | solution.py:134
  178.3 4.9 %collective-permute-start = (f32[1,4,256]{2,0,1:T(1,128)S(1)}, f32[1,4,256]{2,0,1:T(1,128)S(1)}, u32[]{:S(2)}, u32[]{:S(2)}) collective-permute-start(f32[1,4,256]{2,0,1:T(1,128)S(1)} %get-tuple-element.21), channel_id=1, source_target_pairs={{0,1},{1,2},{2,3},{3,4},{4,5},{5,6},{6,7},{7,8},{8,9},{9,10},{10,1... | collective-permute-start | bytes 12296 | tf_op jit(solution)/shard_map/ppermute | solution.py:19
  192.6 3.5 collective-permute-done.3
  197.1 38.0 %all-gather.5.cloned.1.call-done = bf16[512,4,256]{2,0,1:T(8,128)(2,1)} async-done(((bf16[32,4,256]{2,0,1:T(8,128)(2,1)}), bf16[512,4,256]{2,0,1:T(8,128)(2,1)}) %all-gather.5.cloned.1.call-update) | async-done | bytes 1048592 | tf_op jit(solution)/shard_map/all_gather | solution.py:124
  243.7 4.9 %fusion.64 = f32[512,4,2,256]{3,0,2,1:T(8,128)S(1)} fusion(bf16[4,2,256,512]{3,2,1,0:T(8,128)(2,1)S(1)} %bitcast.125), kind=kOutput, calls=%fused_computation.75 | convolution fusion | flops 1078198272 | bytes 6291456 | tf_op jit(solution)/shard_map/dot_general | solution.py:128
  248.6 4.9 %fusion.70 = f32[512,4,2,256]{3,0,2,1:T(8,128)S(1)} fusion(bf16[4,2,256,512]{3,2,1,0:T(8,128)(2,1)S(1)} %bitcast.126), kind=kOutput, calls=%fused_computation.77 | convolution fusion | flops 1077936128 | bytes 6291456 | tf_op jit(solution)/shard_map/dot_general | solution.py:127
  254.6 23.9 %convert_bitcast_fusion = bf16[512,4,2,256]{3,1,2,0:T(4,128)(2,1)} fusion(f32[512,32,256]{2,1,0:T(8,128)} %convert_element_type.111, f32[512,32,256]{2,1,0:T(8,128)} %broadcast_multiply_fusion, bf16[512,32,2,256]{3,2,1,0:T(2,128)(2,1)} %param.6, bf16[512,4,2,256]{3,0,2,1:T(8,128)(2,1)S(1)} %pad_maximum_fusion.1, f32[32,4]{0,1:T(4,128)S(1)} %copy-done.2), kind=kOutput, calls=%fused_computation.56 | convolution fusion | flops 176160896 | bytes 54526464 | tf_op jit(solution)/shard_map/cs,kczl->kszl/dot_general | solution.py:78
  278.6 3.0 copy.48
  281.5 7.3 %fusion.35 = f32[512,4,2,256]{0,3,2,1:T(8,128)S(1)} fusion(bf16[512,4,2,256]{0,3,2,1:T(8,128)(2,1)S(1)} %copy.48), kind=kOutput, calls=%fused_computation.48 | convolution fusion | flops 1078198272 | bytes 6291456 | tf_op jit(solution)/shard_map/dot_general | solution.py:60
  288.9 7.5 %fusion.37 = f32[512,4,2,256]{0,3,2,1:T(8,128)S(1)} fusion(bf16[512,4,2,256]{0,3,2,1:T(8,128)(2,1)S(1)} %copy.48), kind=kOutput, calls=%fused_computation.50 | convolution fusion | flops 1077936128 | bytes 6291456 | tf_op jit(solution)/shard_map/dot_general | solution.py:59
  299.8 58.6 %reduce-scatter.5.cloned.1.call-done = f32[32,4,256]{2,0,1:T(8,128)} async-done(((f32[512,4,256]{2,0,1:T(8,128)}), f32[32,4,256]{2,0,1:T(8,128)}) %reduce-scatter.5.cloned.1.call-update) | async-done | bytes 131088 | tf_op jit(solution)/shard_map/reduce_scatter | solution.py:134
  359.4 4.9 %collective-permute-start.4 = (f32[1,4,256]{2,0,1:T(1,128)S(1)}, f32[1,4,256]{2,0,1:T(1,128)S(1)}, u32[]{:S(2)}, u32[]{:S(2)}) collective-permute-start(f32[1,4,256]{2,0,1:T(1,128)S(1)} %get-tuple-element.17), channel_id=1, source_target_pairs={{0,1},{1,2},{2,3},{3,4},{4,5},{5,6},{6,7},{7,8},{8,9},{9,10},{10,1... | collective-permute-start | bytes 12296 | tf_op jit(solution)/shard_map/ppermute | solution.py:19
  366.2 3.0 collective-permute-done.5
  373.7 3.5 collective-permute-done.7
  (72 shorter events, 47.7 us)
Async XLA Ops:
  6.5 43.5 %all-gather.3.cloned.1.call-start = ((), (), s32[]{:S(2)}) async-start(), calls=%async_computation.2 | async-start | bytes 1114112 | tf_op jit(solution)/shard_map/all_gather | solution.py:124
  8.1 12.5 %copy-start.6 = (s32[32]{0:T(128)S(1)}, s32[32]{0:T(128)}, u32[]{:S(2)}) copy-start(s32[32]{0:T(128)} %param.9) | copy-start | bytes 388
  8.1 169.2 %reduce-scatter.3.cloned.1.call-start = ((), (), s32[]{:S(2)}) async-start(), calls=%async_computation.3 | async-start | bytes 2228224 | tf_op jit(solution)/shard_map/reduce_scatter | solution.py:134
  60.5 6.7 %copy-start = (bf16[2048,512]{1,0:T(8,128)(2,1)S(1)}, bf16[2048,512]{1,0:T(8,128)(2,1)}, u32[]{:S(2)}) copy-start(bf16[2048,512]{1,0:T(8,128)(2,1)} %copy.58) | copy-start | bytes 6291460
  73.0 0.7 copy-start.2
  118.6 58.7 %copy-start.1 = (f32[32,4,256]{2,1,0:T(4,128)S(1)}, f32[32,4,256]{2,1,0:T(4,128)}, u32[]{:S(2)}) copy-start(f32[32,4,256]{2,1,0:T(4,128)} %param.11) | copy-start | bytes 393220
  118.6 66.4 %copy-start.5 = (s32[4,2]{0,1:T(2,128)S(1)}, s32[4,2]{0,1:T(2,128)}, u32[]{:S(2)}) copy-start(s32[4,2]{0,1:T(2,128)} %param.10) | copy-start | bytes 100
  118.7 116.4 %all-gather.5.cloned.1.call-start = ((), (), s32[]{:S(2)}) async-start(), calls=%async_computation.4 | async-start | bytes 1114112 | tf_op jit(solution)/shard_map/all_gather | solution.py:124
  178.3 6.8 %collective-permute-start = (f32[1,4,256]{2,0,1:T(1,128)S(1)}, f32[1,4,256]{2,0,1:T(1,128)S(1)}, u32[]{:S(2)}, u32[]{:S(2)}) collective-permute-start(f32[1,4,256]{2,0,1:T(1,128)S(1)} %get-tuple-element.21), channel_id=1, source_target_pairs={{0,1},{1,2},{2,3},{3,4},{4,5},{5,6},{6,7},{7,8},{8,9},{9,10},{10,1... | collective-permute-start | bytes 12296 | tf_op jit(solution)/shard_map/ppermute | solution.py:19
  183.1 4.9 %collective-permute-start.1 = (f32[1,4,256]{2,0,1:T(1,128)S(1)}, f32[1,4,256]{2,0,1:T(1,128)S(1)}, u32[]{:S(2)}, u32[]{:S(2)}) collective-permute-start(f32[1,4,256]{2,0,1:T(1,128)S(1)} %get-tuple-element.22), channel_id=1, source_target_pairs={{1,0},{2,1},{3,2},{4,3},{5,4},{6,5},{7,6},{8,7},{9,8},{10,9},{11,1... | collective-permute-start | bytes 12296 | tf_op jit(solution)/shard_map/ppermute | solution.py:21
  188.3 4.4 %collective-permute-start.2 = (f32[2,4,256]{2,0,1:T(2,128)S(1)}, f32[2,4,256]{2,0,1:T(2,128)S(1)}, u32[]{:S(2)}, u32[]{:S(2)}) collective-permute-start(f32[2,4,256]{2,0,1:T(2,128)S(1)} %get-tuple-element.19), channel_id=1, source_target_pairs={{0,1},{1,2},{2,3},{3,4},{4,5},{5,6},{6,7},{7,8},{8,9},{9,10},{10,1... | collective-permute-start | bytes 24584 | tf_op jit(solution)/shard_map/ppermute | solution.py:19
  190.2 5.9 %collective-permute-start.3 = (f32[2,4,256]{2,0,1:T(2,128)S(1)}, f32[2,4,256]{2,0,1:T(2,128)S(1)}, u32[]{:S(2)}, u32[]{:S(2)}) collective-permute-start(f32[2,4,256]{2,0,1:T(2,128)S(1)} %get-tuple-element.20), channel_id=1, source_target_pairs={{1,0},{2,1},{3,2},{4,3},{5,4},{6,5},{7,6},{8,7},{9,8},{10,9},{11,1... | collective-permute-start | bytes 24584 | tf_op jit(solution)/shard_map/ppermute | solution.py:21
  192.6 4.3 %copy-start.3 = (f32[4]{0:T(128)}, f32[4]{0:T(128)S(1)}, u32[]{:S(2)}) copy-start(f32[4]{0:T(128)S(1)} %get-tuple-element.26) | copy-start | bytes 52
  197.0 161.4 %reduce-scatter.5.cloned.1.call-start = ((), (), s32[]{:S(2)}) async-start(), calls=%async_computation.5 | async-start | bytes 2228224 | tf_op jit(solution)/shard_map/reduce_scatter | solution.py:134
  299.7 77.5 %copy-start.4 = (f32[4]{0:T(128)S(1)}, f32[4]{0:T(128)}, u32[]{:S(2)}) copy-start(f32[4]{0:T(128)} %copy-done.3) | copy-start | bytes 52
  359.4 6.8 %collective-permute-start.4 = (f32[1,4,256]{2,0,1:T(1,128)S(1)}, f32[1,4,256]{2,0,1:T(1,128)S(1)}, u32[]{:S(2)}, u32[]{:S(2)}) collective-permute-start(f32[1,4,256]{2,0,1:T(1,128)S(1)} %get-tuple-element.17), channel_id=1, source_target_pairs={{0,1},{1,2},{2,3},{3,4},{4,5},{5,6},{6,7},{7,8},{8,9},{9,10},{10,1... | collective-permute-start | bytes 12296 | tf_op jit(solution)/shard_map/ppermute | solution.py:19
  364.2 4.9 %collective-permute-start.5 = (f32[1,4,256]{2,0,1:T(1,128)S(1)}, f32[1,4,256]{2,0,1:T(1,128)S(1)}, u32[]{:S(2)}, u32[]{:S(2)}) collective-permute-start(f32[1,4,256]{2,0,1:T(1,128)S(1)} %get-tuple-element.18), channel_id=1, source_target_pairs={{1,0},{2,1},{3,2},{4,3},{5,4},{6,5},{7,6},{8,7},{9,8},{10,9},{11,1... | collective-permute-start | bytes 12296 | tf_op jit(solution)/shard_map/ppermute | solution.py:21
  369.4 4.3 %collective-permute-start.6 = (f32[2,4,256]{2,0,1:T(2,128)S(1)}, f32[2,4,256]{2,0,1:T(2,128)S(1)}, u32[]{:S(2)}, u32[]{:S(2)}) collective-permute-start(f32[2,4,256]{2,0,1:T(2,128)S(1)} %get-tuple-element.15), channel_id=1, source_target_pairs={{0,1},{1,2},{2,3},{3,4},{4,5},{5,6},{6,7},{7,8},{8,9},{9,10},{10,1... | collective-permute-start | bytes 24584 | tf_op jit(solution)/shard_map/ppermute | solution.py:19
  371.3 5.9 %collective-permute-start.7 = (f32[2,4,256]{2,0,1:T(2,128)S(1)}, f32[2,4,256]{2,0,1:T(2,128)S(1)}, u32[]{:S(2)}, u32[]{:S(2)}) collective-permute-start(f32[2,4,256]{2,0,1:T(2,128)S(1)} %get-tuple-element.16), channel_id=1, source_target_pairs={{1,0},{2,1},{3,2},{4,3},{5,4},{6,5},{7,6},{8,7},{9,8},{10,9},{11,1... | collective-permute-start | bytes 24584 | tf_op jit(solution)/shard_map/ppermute | solution.py:21
Sparse Core Ops, SparseCore 0:
  9.5 40.4 all-gather.2
  118.8 58.4 reduce-scatter.2
  197.1 37.8 all-gather.4
  299.9 58.4 reduce-scatter.4
where the time goes:
time: 391 us; the launch traced here: 385 us
  waiting for transfers between devices  186 us (48%)
  matrix products  104 us (27%)
  other arithmetic  33.6 us (9%)
  local copies, waits for them, and re-layouts  24.9 us (6%)
  starting transfers between devices  22.4 us (6%)
  between operations  13.8 us (4%)
    reduce_scatter x2, waiting for transfers between devices, body(): lax.psum_scatter(inverse_rows(row_real, row_imag, packed_grad, col_back,...  117 us
    all_gather x2, waiting for transfers between devices, body(): gathered = lax.all_gather(rounded, 'chan', axis=0, tiled=True)  55.7 us
    dot_general x2, matrix products, block_gradient(): summed = jnp.einsum('cs,kczl->kszl', mix_block, weighted)  48.1 us
    dot_general x2, matrix products, inverse_rows(): jnp.dot(row_real, packed_grad, preferred_element_type=jnp.float32)  14.8 us
    dot_general x2, matrix products, inverse_rows(): jnp.dot(row_imag, packed_grad, preferred_element_type=jnp.float32)  14.7 us
    ppermute x4, starting transfers between devices, padded_2(): lax.ppermute(tail, axis, [(i, (i + 1) % count) for i in range(ends)])  13.6 us
    ppermute x4, waiting for transfers between devices, padded_2(): lax.ppermute(head, axis, [((i + 1) % count, i) for i in range(ends)])  12.9 us
    mul x1, other arithmetic, block_gradient(): weighted = weight[None, :, None, None] * beam_gain * residual  11.7 us
  transfers between devices with their start and end apart: 12, of which 8 were waited for; matrix products, arithmetic and copies ran while one was open for 6% of the time, Pallas kernels for 0%

commit v1 on v0

--- a/solution.py
+++ b/solution.py
@@ -1,8 +1,13 @@
+import functools
 import math
 
 import jax
 import jax.numpy as jnp
+import ml_dtypes
+import numpy as np
 from jax import lax
+from jax.experimental import pallas as pl
+from jax.experimental.pallas import tpu as pltpu
 from jax.sharding import PartitionSpec as P
 
 ITERS = 2
@@ -108,7 +113,7 @@
     )
 
 
-def body(sky_data, beam_gains, mixing, noise_levels, threshold_levels, start_sources):
+def plain_body(sky_data, beam_gains, mixing, noise_levels, threshold_levels, start_sources):
     strip_rows, source_count, col_count = start_sources.shape
     full_rows = strip_rows * lax.axis_size("chan")
     row_real, row_imag = dft_tables(full_rows)
@@ -146,6 +151,281 @@
     return sources
 
 
+BF16 = jnp.bfloat16
+F32 = jnp.float32
+VMEM_LIMIT = 56 * 1024 * 1024
+PAIRS = [(s, t) for s in range(4) for t in range(s, 4)]
+PAIR_OF = {}
+for number, (first, second) in enumerate(PAIRS):
+    PAIR_OF[first, second] = number
+    PAIR_OF[second, first] = number
+
+
+def host_tables(length):
+    positions = np.arange(length)
+    angles = (positions[:, None] * positions[None, :] % length) * (2.0 * math.pi / length)
+    norm_factor = 1.0 / math.sqrt(length)
+    return (
+        (np.cos(angles) * norm_factor).astype(np.float32).astype(ml_dtypes.bfloat16),
+        (-np.sin(angles) * norm_factor).astype(np.float32).astype(ml_dtypes.bfloat16),
+    )
+
+
+def smooth_window(x, first_row, row_total, fine, coarse_bound):
+    height, width = x.shape
+    rows = lax.broadcasted_iota(jnp.int32, (height, width), 0) + first_row
+    lanes = lax.broadcasted_iota(jnp.int32, (height, width), 1)
+    inside = (rows >= 0) & (rows < row_total)
+
+    def smooth(v, d):
+        v = 0.25 * (pltpu.roll(v, d, 0) + 2.0 * v + pltpu.roll(v, height - d, 0))
+        left = jnp.where(lanes >= d, pltpu.roll(v, d, 1), 0.0)
+        right = jnp.where(lanes < width - d, pltpu.roll(v, width - d, 1), 0.0)
+        return 0.25 * (left + 2.0 * v + right)
+
+    c1 = jnp.where(inside, smooth(x, 1), 0.0)
+    c2 = smooth(c1, 2)
+    d1 = c1 - c2
+    d0 = x - c1
+    result = c2 + (d1 - jnp.clip(d1, -coarse_bound, coarse_bound)) + (d0 - jnp.clip(d0, -fine, fine))
+    return result[8 : height - 8]
+
+
+def step_kernel(
+    last, s_ref, own_ref, d_ref, h_ref, colcat_ref, colback_ref, fwd_ref, bwd_ref, lam_ref, out_ref,
+    pst, gst, vb, got_core, acc, got_y, fin, got_z, vall, xpad, halo,
+    core_s, core_r, y_s, y_r, z_s, z_r, gz_s, gz_r, gy_s, gy_r, gc_s, gc_r, halo_s, halo_r,
+):
+    blocks, sources, strip, cols = s_ref.shape
+    nrow = blocks * strip
+    me = lax.axis_index("chan")
+    z, y, c = me // 4, (me // 2) % 2, me % 2
+
+    def index(zz, yy, cc):
+        return zz * 4 + yy * 2 + cc
+
+    core_peer = index(z, y, 1 - c)
+    y_peer = index(z, 1 - y, c)
+    z_peers = [index((z + 1 + i) % 4, y, c) for i in range(3)]
+    z_from = [index((z + 3 - i) % 4, y, c) for i in range(3)]
+    right, left = (me + 1) % blocks, (me + blocks - 1) % blocks
+
+    barrier = pltpu.get_barrier_semaphore()
+    greeted = [core_peer, y_peer] + z_peers + ([left, right] if last else [])
+    for peer in greeted:
+        pl.semaphore_signal(barrier, inc=1, device_id={"chan": peer}, device_id_type=pl.DeviceIdType.MESH)
+
+    def remote(src, dst, send, recv, peer):
+        return pltpu.make_async_remote_copy(
+            src_ref=src, dst_ref=dst, send_sem=send, recv_sem=recv,
+            device_id={"chan": peer}, device_id_type=pl.DeviceIdType.MESH,
+        )
+
+    for t in range(sources):
+        rows = s_ref[:, t].reshape(nrow, cols).astype(BF16)
+        p = jnp.dot(rows, colcat_ref[...], preferred_element_type=F32)
+        pst[0:nrow, t * cols : (t + 1) * cols] = p[:, :cols].astype(BF16)
+        pst[nrow:, t * cols : (t + 1) * cols] = p[:, cols:].astype(BF16)
+
+    tile = 128
+
+    @pl.loop(0, nrow // tile)
+    def _(kb):
+        k0 = pl.multiple_of(kb * tile, tile)
+        k1 = pl.multiple_of(nrow + kb * tile, tile)
+        for part, start in ((0, k0), (1, k1)):
+            q = jnp.dot(fwd_ref[pl.ds(start, tile), :], pst[...], preferred_element_type=F32)
+            for s in range(sources):
+                g = d_ref[part, s, pl.ds(k0, tile), :].astype(F32)
+                for t in range(sources):
+                    hh = h_ref[PAIR_OF[s, t], pl.ds(k0, tile), :].astype(F32)
+                    g = g - hh * q[:, t * cols : (t + 1) * cols]
+                gst[pl.ds(start, tile), s * cols : (s + 1) * cols] = g.astype(BF16)
+
+    pl.semaphore_wait(barrier, len(greeted))
+
+    core_copies, y_copies, z_copies = [], [], []
+
+    def do_core(i):
+        zb = (z + 1 + i) % 4
+        r0 = pl.multiple_of(zb * tile, tile)
+        r1 = pl.multiple_of(nrow + zb * tile, tile)
+        ur = jnp.dot(bwd_ref[pl.ds(r0, tile), :], gst[...], preferred_element_type=F32).astype(BF16)
+        ui = jnp.dot(bwd_ref[pl.ds(r1, tile), :], gst[...], preferred_element_type=F32).astype(BF16)
+        for s in range(sources):
+            both = jnp.concatenate([ur[:, s * cols : (s + 1) * cols], ui[:, s * cols : (s + 1) * cols]], axis=1)
+            v = jnp.dot(both, colback_ref[...], preferred_element_type=F32)
+            vb[i, :, :, s] = v.astype(BF16).reshape(2, 2, strip, cols)
+        copy = remote(vb.at[i, :, 1 - c], got_core.at[i], core_s.at[i], core_r.at[i], core_peer)
+        copy.start()
+        core_copies.append(copy)
+
+    def do_y(i):
+        core_copies[i].wait()
+        acc[i] = (vb[i, :, c].astype(F32) + got_core[i].astype(F32)).astype(BF16)
+        copy = remote(acc.at[i, 1 - y], got_y.at[i], y_s.at[i], y_r.at[i], y_peer)
+        copy.start()
+        y_copies.append(copy)
+
+    def do_z(i):
+        y_copies[i].wait()
+        fin[i] = (acc[i, y].astype(F32) + got_y[i].astype(F32)).astype(BF16)
+        copy = remote(fin.at[i], got_z.at[i], z_s.at[i], z_r.at[i], z_peers[i])
+        copy.start()
+        z_copies.append(copy)
+
+    do_core(0)
+    do_core(1)
+    do_y(0)
+    do_core(2)
+    do_y(1)
+    do_z(0)
+    do_core(3)
+    do_y(2)
+    do_z(1)
+    do_y(3)
+    do_z(2)
+    y_copies[3].wait()
+    total = acc[3, y].astype(F32) + got_y[3].astype(F32)
+    for i in range(3):
+        z_copies[i].wait()
+        total = total + got_z[i].astype(F32)
+
+    def bound(s, j):
+        return lam_ref[s, j]
+
+    if not last:
+        vall[me] = total.astype(BF16)
+        gz, gy, gc = [], [], []
+        for i in range(3):
+            copy = remote(vall.at[me], vall.at[me], gz_s.at[i], gz_r.at[i], z_peers[i])
+            copy.start()
+            gz.append(copy)
+
+        def to_core(src, j):
+            copy = remote(vall.at[src], vall.at[src], gc_s.at[j], gc_r.at[j], core_peer)
+            copy.start()
+            gc.append(copy)
+
+        held = [me] + z_from
+        for j in range(4):
+            if j > 0:
+                gz[j - 1].wait_recv()
+            copy = remote(vall.at[held[j]], vall.at[held[j]], gy_s.at[j], gy_r.at[j], y_peer)
+            copy.start()
+            gy.append(copy)
+            to_core(held[j], j)
+        for j in range(4):
+            gy[j].wait_recv()
+            zz = (z + 4 - j) % 4
+            to_core(index(zz, 1 - y, c), 4 + j)
+        for copy in gc:
+            copy.wait_recv()
+        for copy in gz + gy + gc:
+            copy.wait_send()
+        xpad[:, 0:16] = jnp.zeros((sources, 16, cols), F32)
+        xpad[:, nrow + 16 :] = jnp.zeros((sources, 16, cols), F32)
+
+        @pl.loop(0, blocks)
+        def _(b):
+            xpad[:, pl.ds(pl.multiple_of(16 + b * strip, 16), strip)] = s_ref[b].astype(F32) + vall[b].astype(F32)
+
+        xpad[:, pl.ds(pl.multiple_of(16 + me * strip, 16), strip)] = own_ref[...] + total
+
+        @pl.loop(0, blocks)
+        def _(b):
+            start = pl.multiple_of(8 + b * strip, 8)
+            for s in range(sources):
+                x = xpad[s, pl.ds(start, strip + 16), :]
+                out_ref[b, s] = smooth_window(x, b * strip - 8, nrow, bound(s, 0), bound(s, 1))
+    else:
+        mine = s_ref[me]
+        vall[me] = total.astype(BF16)
+        half = strip // 2
+        to_right = remote(vall.at[me, :, half:strip], halo.at[0], halo_s.at[0], halo_r.at[0], right)
+        to_left = remote(vall.at[me, :, 0:half], halo.at[1], halo_s.at[1], halo_r.at[1], left)
+        to_right.start()
+        to_left.start()
+        xpad[:, 16 : 16 + strip] = mine + total
+        above = s_ref[left, :, half:strip]
+        below = s_ref[right, :, 0:half]
+        to_right.wait()
+        to_left.wait()
+        above = above + halo[0].astype(F32)
+        below = below + halo[1].astype(F32)
+        xpad[:, 0:16] = jnp.where(me > 0, above, 0.0)
+        xpad[:, 16 + strip : 32 + strip] = jnp.where(me < blocks - 1, below, 0.0)
+        for s in range(sources):
+            x = xpad[s, 8 : 24 + strip, :]
+            out_ref[s] = smooth_window(x, me * strip - 8, nrow, bound(s, 0), bound(s, 1))
+
+
+def step(last, s_full, own, dd, hh, tables, lam):
+    blocks, sources, strip, cols = s_full.shape
+    nrow = blocks * strip
+    vm = pl.BlockSpec(memory_space=pltpu.VMEM)
+    dma = pltpu.SemaphoreType.DMA
+    block = (sources, strip, cols)
+    return pl.pallas_call(
+        functools.partial(step_kernel, last),
+        out_shape=jax.ShapeDtypeStruct(block if last else (blocks,) + block, F32),
+        in_specs=[vm] * 8 + [pl.BlockSpec(memory_space=pltpu.SMEM)],
+        out_specs=vm,
+        scratch_shapes=[
+            pltpu.VMEM((2 * nrow, sources * cols), BF16),
+            pltpu.VMEM((2 * nrow, sources * cols), BF16),
+            pltpu.VMEM((4, 2, 2) + block, BF16),
+            pltpu.VMEM((4, 2) + block, BF16),
+            pltpu.VMEM((4, 2) + block, BF16),
+            pltpu.VMEM((4,) + block, BF16),
+            pltpu.VMEM((3,) + block, BF16),
+            pltpu.VMEM((3,) + block, BF16),
+            pltpu.VMEM((blocks,) + block, BF16),
+            pltpu.VMEM((sources, (strip if last else nrow) + 32, cols), F32),
+            pltpu.VMEM((2, sources, 16, cols), BF16),
+            dma((4,)), dma((4,)), dma((4,)), dma((4,)), dma((3,)), dma((3,)),
+            dma((3,)), dma((3,)), dma((4,)), dma((4,)), dma((8,)), dma((8,)),
+            dma((2,)), dma((2,)),
+        ],
+        compiler_params=pltpu.CompilerParams(
+            collective_id=1 if last else 0, has_side_effects=True, vmem_limit_bytes=VMEM_LIMIT
+        ),
+    )(s_full, own, dd, hh, *tables, lam)
+
+
+def channel_sums(sky_data, beam_gains, mixing, noise_levels):
+    weighted = mixing * (noise_levels.astype(F32) * 0.25)[:, None]
+    beam = beam_gains.astype(F32)
+    gd = (beam[:, :, None, :] * sky_data.astype(F32)).astype(BF16)
+    gg = (beam * beam).astype(BF16)
+    pair = jnp.stack([weighted[:, s] * mixing[:, t] for s, t in PAIRS], axis=1)
+    dd = jnp.einsum("cs,kczl->zskl", weighted.astype(BF16), gd, preferred_element_type=F32)
+    hh = jnp.einsum("cp,kcl->pkl", pair.astype(BF16), gg, preferred_element_type=F32)
+    return dd.astype(BF16), hh.astype(BF16)
+
+
+def body(sky_data, beam_gains, mixing, noise_levels, threshold_levels, start_sources):
+    strip, sources, cols = start_sources.shape
+    blocks = lax.axis_size("chan")
+    if blocks != 16 or strip != 32 or sources != 4 or cols % 128:
+        return plain_body(sky_data, beam_gains, mixing, noise_levels, threshold_levels, start_sources)
+    row_real, row_imag = host_tables(strip * blocks)
+    col_real, col_imag = host_tables(cols)
+    tables = [
+        jnp.asarray(np.concatenate([col_real, col_imag], axis=1)),
+        jnp.asarray(np.concatenate([col_real, col_imag], axis=0)),
+        jnp.asarray(np.block([[row_real, -row_imag], [row_imag, row_real]])),
+        jnp.asarray(np.block([[row_real, row_imag], [-row_imag, row_real]])),
+    ]
+    lam = threshold_levels.astype(F32) * 0.05
+    own = jnp.swapaxes(start_sources, 0, 1)
+    s_full = lax.all_gather(own.astype(BF16), "chan", axis=0)
+    dd, hh = channel_sums(sky_data, beam_gains, mixing, noise_levels)
+    s_full = step(False, s_full, own, dd, hh, tables, lam)
+    result = step(True, s_full, own, dd, hh, tables, lam)
+    return jnp.swapaxes(result, 0, 1)
+
+
 def solution(mesh):
     return jax.shard_map(
         body,

time: 391 us -> 145 us (0.37); the launches traced: 385 us -> 143 us
  waiting for transfers between devices: 186 us -> 0.02 us
  matrix products: 104 us -> 13.1 us
  Pallas kernels: 0 us -> 72.8 us
  starting transfers between devices: 22.4 us -> 0.01 us
  local copies, waits for them, and re-layouts: 24.9 us -> 9.15 us
    reduce_scatter x2 -> x0, waiting for transfers between devices: 117 us -> none  [body(): lax.psum_scatter(inverse_rows(row_real, row_imag, packed_grad, col_back,...]
    dot_general x14 -> x2, matrix products: 104 us -> 13.1 us  [the longest x1 8.13 us: channel_sums(): jnp.einsum('cs,kczl->zskl', weighted.astype(BF16), gd, preferred_element_...]
    pallas_call x0 -> x2, Pallas kernels: none -> 72.8 us  [step(): pl.pallas_call(functools.partial(step_kernel, last), out_shape=jax.ShapeD...]
    all_gather x2 -> x1, waiting for transfers between devices: 55.7 us -> 0.01 us  [body(): s_full = lax.all_gather(own.astype(BF16), 'chan', axis=0)]
    ppermute x8 -> x0, starting transfers between devices: 22.2 us -> none  [the longest x4 13.6 us: padded_2(): lax.ppermute(tail, axis, [(i, (i + 1) % count) for i in range(ends)])]
    convert_element_type x4 -> x2, other arithmetic: 14.8 us -> 34.1 us  [the longest x1 22.8 us: channel_sums(): gd = (beam[:, :, None, :] * sky_data.astype(F32)).astype(BF16)]
    ppermute x8 -> x0, waiting for transfers between devices: 12.9 us -> none  [the longest x4 12.9 us: padded_2(): lax.ppermute(head, axis, [((i + 1) % count, i) for i in range(ends)])]
    mul x9 -> x3, other arithmetic: 12.2 us -> 0.6 us  [the longest x1 0.59 us: body(): lam = threshold_levels.astype(F32) * 0.05]
  transfers between devices with their start and end apart: 12 -> 1, of which waited for: 8 -> 0; matrix products, arithmetic and copies ran while one was open for 6% -> 38% of each run, Pallas kernels for 0% -> 0%
where the time goes in v1:
time: 145 us; the launch traced here: 143 us
  Pallas kernels  72.8 us (50%)
  other arithmetic  34.7 us (24%)
  between operations  13.5 us (9%)
  matrix products  13.1 us (9%)
  local copies, waits for them, and re-layouts  9.15 us (6%)
    pallas_call x2, Pallas kernels, step(): pl.pallas_call(functools.partial(step_kernel, last), out_shape=jax.ShapeD...  72.8 us
    convert_element_type x1, other arithmetic, channel_sums(): gd = (beam[:, :, None, :] * sky_data.astype(F32)).astype(BF16)  22.8 us
    convert_element_type x1, other arithmetic, channel_sums(): beam = beam_gains.astype(F32)  11.3 us
    dot_general x1, matrix products, channel_sums(): jnp.einsum('cs,kczl->zskl', weighted.astype(BF16), gd, preferred_element_...  8.13 us
    dot_general x1, matrix products, channel_sums(): jnp.einsum('cp,kcl->pkl', pair.astype(BF16), gg, preferred_element_type=F32)  5.01 us
    unnamed x9, local copies, waits for them, and re-layouts  3.26 us
  transfers between devices with their start and end apart: 1, of which 0 were waited for; matrix products, arithmetic and copies ran while one was open for 38% of the time, Pallas kernels for 0%

profile of v1, /device:TPU:1, one launch (start us, length us, event | category | flops | bytes accessed | tf_op | source)
XLA Modules:
  0.0 143.3 jit_solution(17936463039623747182)
XLA Ops:
  6.5 0.0 copy-start.2
  6.5 0.0 all-gather.3.cloned.1.call-start
  6.5 1.6 %copy.36 = bf16[32,4,256]{2,0,1:T(8,128)(2,1)} copy(f32[32,4,256]{2,1,0:T(4,128)} %param.15) | data formatting | bytes 196608 | tf_op args[5]
  8.1 0.0 all-gather.3.cloned.1.call-update
  8.1 1.6 %copy.35 = f32[32,4,256]{2,0,1:T(8,128)} copy(f32[32,4,256]{2,1,0:T(4,128)} %param.15) | data formatting | bytes 262144 | tf_op args[5]
  9.7 11.3 %convert_element_type.34 = f32[512,32,256]{2,1,0:T(8,128)} convert(bf16[512,32,256]{2,1,0:T(8,128)(2,1)} %param.11) | non-fusion elementwise | flops 4194304 | bytes 25165824 | tf_op jit(solution)/shard_map/convert_element_type | solution.py:398
  21.0 0.0 copy-done.2
  21.0 0.0 copy-start
  21.0 22.8 %multiply_convert_fusion = bf16[512,32,2,256]{3,2,1,0:T(2,128)(2,1)} fusion(bf16[512,32,2,256]{3,2,1,0:T(2,128)(2,1)} %param.10, f32[512,32,256]{2,1,0:T(8,128)} %convert_element_type.34), kind=kLoop, calls=%fused_computation | loop fusion | flops 25165824 | bytes 50331648 | tf_op jit(solution)/shard_map/convert_element_type | solution.py:399
  43.8 0.0 copy-done
  43.9 8.1 %fusion = bf16[512,2,256,4]{2,3,1,0:T(4,128)(2,1)S(1)} fusion(bf16[512,32,2,256]{3,2,1,0:T(2,128)(2,1)} %multiply_convert_fusion, f32[32,4]{0,1:T(4,128)S(1)} %broadcast_multiply_fusion), kind=kOutput, calls=%fused_computation.1 | convolution fusion | flops 67108992 | bytes 18874880 | tf_op jit(solution)/shard_map/cs,kczl->zskl/dot_general | solution.py:402
  52.0 0.0 copy-start.1
  52.0 1.7 %copy.34 = bf16[512,2,256,4]{2,0,3,1:T(8,128)(2,1)} copy(bf16[512,2,256,4]{2,3,1,0:T(4,128)(2,1)S(1)} %fusion) | data formatting | bytes 4194304 | tf_op jit(solution)/shard_map/cs,kczl->zskl/dot_general | solution.py:402
  53.8 0.1 stack.3
  53.8 5.0 %fusion.2 = bf16[10,512,256]{2,0,1:T(8,128)(2,1)S(1)} fusion(bf16[512,32,256]{2,1,0:T(8,128)(2,1)} %param.11, bf16[32,10]{0,1:T(8,128)(2,1)S(1)} %stack.3), kind=kOutput, calls=%fused_computation.4 | convolution fusion | flops 96468992 | bytes 11010688 | tf_op jit(solution)/shard_map/cp,kcl->pkl/dot_general | solution.py:403
  58.8 2.4 %copy.33.h_ref = bf16[10,512,256]{2,1,0:T(8,128)(2,1)} copy(bf16[10,512,256]{2,0,1:T(8,128)(2,1)S(1)} %fusion.2) | data formatting | bytes 5242880 | tf_op jit(solution)/shard_map/cp,kcl->pkl/dot_general | solution.py:403
  61.3 0.0 copy-done.1
  61.3 0.1 copy.21
  61.4 0.6 convert_multiply_fusion.lam_ref
  62.0 0.0 all-gather.3.cloned.1.call-done
  62.0 44.9 %shard_map.100.s_ref = f32[16,4,32,256]{3,2,1,0:T(8,128)} custom-call(bf16[16,4,32,256]{3,2,1,0:T(8,128)(2,1)} %bitcast.23, f32[4,32,256]{2,1,0:T(8,128)} %bitcast.21, bf16[2,4,512,256]{3,2,1,0:T(8,128)(2,1)} %bitcast.19, bf16[10,512,256]{2,1,0:T(8,128)(2,1)} %copy.33.h_ref, bf16[256,512]{1,0:T(8,128)(2,1)} %constant.12.clone.colcat_ref, ...), custom_call_target="tpu_custom_call" | custom-call | tf_op jit(solution)/shard_map/pallas_call | solution.py:369
  106.9 27.9 %shard_map.101 = f32[4,32,256]{2,1,0:T(8,128)} custom-call(f32[16,4,32,256]{3,2,1,0:T(8,128)} %shard_map.100.s_ref, f32[4,32,256]{2,1,0:T(8,128)} %bitcast.22, bf16[2,4,512,256]{3,2,1,0:T(8,128)(2,1)} %bitcast.20, bf16[10,512,256]{2,1,0:T(8,128)(2,1)} %copy.33.h_ref, bf16[256,512]{1,0:T(8,128)(2,1)} %constant.12.clone.colcat_ref, ...), custom_call_target="tpu_custom_call" | custom-call | tf_op jit(solution)/shard_map/pallas_call | solution.py:369
  134.8 1.6 %copy.22 = f32[32,4,256]{2,1,0:T(4,128)} copy(f32[32,4,256]{2,0,1:T(8,128)} %bitcast.24) | data formatting | bytes 262144 | tf_op jit(solution)/shard_map/transpose | solution.py:426
  (4 shorter events, 0.0 us)
Async XLA Ops:
  6.5 14.5 %copy-start.2 = (s32[32]{0:T(128)S(1)}, s32[32]{0:T(128)}, u32[]{:S(2)}) copy-start(s32[32]{0:T(128)} %param.13) | copy-start | bytes 388
  6.5 55.4 %all-gather.3.cloned.1.call-start = ((), (), s32[]{:S(2)}) async-start(), calls=%async_computation | async-start | bytes 1114112 | tf_op jit(solution)/shard_map/all_gather | solution.py:422
  21.0 22.8 %copy-start = (f32[32,4]{0,1:T(4,128)S(1)}, f32[32,4]{0,1:T(4,128)}, u32[]{:S(2)}) copy-start(f32[32,4]{0,1:T(4,128)} %param.12) | copy-start | bytes 1540
  52.0 9.3 %copy-start.1 = (s32[4,2]{0,1:T(2,128)S(1)}, s32[4,2]{0,1:T(2,128)}, u32[]{:S(2)}) copy-start(s32[4,2]{0,1:T(2,128)} %param.14) | copy-start | bytes 100
Sparse Core Ops, SparseCore 0:
  9.5 40.4 all-gather.2

commit v2 on v1

--- a/solution.py
+++ b/solution.py
@@ -192,10 +192,18 @@
 
 
 def step_kernel(
-    last, s_ref, own_ref, d_ref, h_ref, colcat_ref, colback_ref, fwd_ref, bwd_ref, lam_ref, out_ref,
-    pst, gst, vb, got_core, acc, got_y, fin, got_z, vall, xpad, halo,
-    core_s, core_r, y_s, y_r, z_s, z_r, gz_s, gz_r, gy_s, gy_r, gc_s, gc_r, halo_s, halo_r,
+    last, s_ref, own_ref, d_ref, h_ref, colcat_ref, colback_ref, fwd_ref, bwd_ref, lam_ref, *rest
 ):
+    if last:
+        (out_ref,), rest = rest[:1], rest[1:]
+        dsum_ref, hsum_ref, got_d, got_h = d_ref, h_ref, None, None
+    else:
+        (out_ref, dsum_ref, hsum_ref), rest = rest[:3], rest[3:]
+        (got_d, got_h), rest = rest[:2], rest[2:]
+    (
+    qst, pst, gst, vb, got_core, acc, got_y, fin, got_z, vall, xpad, halo,
+    core_s, core_r, y_s, y_r, z_s, z_r, gz_s, gz_r, gy_s, gy_r, gc_s, gc_r, halo_s, halo_r, half_s, half_r,
+    ) = rest
     blocks, sources, strip, cols = s_ref.shape
     nrow = blocks * strip
     me = lax.axis_index("chan")
@@ -221,6 +229,15 @@
             device_id={"chan": peer}, device_id_type=pl.DeviceIdType.MESH,
         )
 
+    half_k = nrow // 2
+    if not last:
+        pl.semaphore_wait(barrier, len(greeted))
+        other = pl.ds(pl.multiple_of((1 - c) * half_k, half_k), half_k)
+        swap_d = remote(d_ref.at[:, :, other, :], got_d, half_s.at[0], half_r.at[0], core_peer)
+        swap_h = remote(h_ref.at[:, other, :], got_h, half_s.at[1], half_r.at[1], core_peer)
+        swap_d.start()
+        swap_h.start()
+
     for t in range(sources):
         rows = s_ref[:, t].reshape(nrow, cols).astype(BF16)
         p = jnp.dot(rows, colcat_ref[...], preferred_element_type=F32)
@@ -228,21 +245,45 @@
         pst[nrow:, t * cols : (t + 1) * cols] = p[:, cols:].astype(BF16)
 
     tile = 128
+    mine_k = pl.multiple_of(c * nrow, nrow)
 
     @pl.loop(0, nrow // tile)
     def _(kb):
         k0 = pl.multiple_of(kb * tile, tile)
-        k1 = pl.multiple_of(nrow + kb * tile, tile)
-        for part, start in ((0, k0), (1, k1)):
-            q = jnp.dot(fwd_ref[pl.ds(start, tile), :], pst[...], preferred_element_type=F32)
+        rows = fwd_ref[pl.ds(pl.multiple_of(mine_k + k0, tile), tile), :]
+        qst[pl.ds(k0, tile), :] = jnp.dot(rows, pst[...], preferred_element_type=F32)
+
+    if not last:
+        swap_d.wait()
+        swap_h.wait()
+    thin = 16
+
+    @pl.loop(0, half_k // thin)
+    def _(kb):
+        k0 = pl.multiple_of(kb * thin, thin)
+        here = pl.ds(k0, thin)
+        if last:
+            h = [h_ref[p, here, :].astype(F32) for p in range(len(PAIRS))]
+        else:
+            whole = pl.ds(pl.multiple_of(c * half_k + k0, thin), thin)
+            h = [(h_ref[p, whole, :].astype(F32) + got_h[p, here, :].astype(F32)) for p in range(len(PAIRS))]
+            for p in range(len(PAIRS)):
+                hsum_ref[p, here, :] = h[p].astype(BF16)
+        for part in range(2):
+            rows = pl.ds(pl.multiple_of(part * half_k + k0, thin), thin)
+            q = [qst[rows, t * cols : (t + 1) * cols] for t in range(sources)]
             for s in range(sources):
-                g = d_ref[part, s, pl.ds(k0, tile), :].astype(F32)
+                if last:
+                    g = d_ref[part, s, here, :].astype(F32)
+                else:
+                    g = d_ref[part, s, whole, :].astype(F32) + got_d[part, s, here, :].astype(F32)
+                    dsum_ref[part, s, here, :] = g.astype(BF16)
                 for t in range(sources):
-                    hh = h_ref[PAIR_OF[s, t], pl.ds(k0, tile), :].astype(F32)
-                    g = g - hh * q[:, t * cols : (t + 1) * cols]
-                gst[pl.ds(start, tile), s * cols : (s + 1) * cols] = g.astype(BF16)
-
-    pl.semaphore_wait(barrier, len(greeted))
+                    g = g - h[PAIR_OF[s, t]] * q[t]
+                gst[rows, s * cols : (s + 1) * cols] = g.astype(BF16)
+
+    if last:
+        pl.semaphore_wait(barrier, len(greeted))
 
     core_copies, y_copies, z_copies = [], [], []
 
@@ -250,8 +291,8 @@
         zb = (z + 1 + i) % 4
         r0 = pl.multiple_of(zb * tile, tile)
         r1 = pl.multiple_of(nrow + zb * tile, tile)
-        ur = jnp.dot(bwd_ref[pl.ds(r0, tile), :], gst[...], preferred_element_type=F32).astype(BF16)
-        ui = jnp.dot(bwd_ref[pl.ds(r1, tile), :], gst[...], preferred_element_type=F32).astype(BF16)
+        ur = jnp.dot(bwd_ref[pl.ds(r0, tile), pl.ds(mine_k, nrow)], gst[...], preferred_element_type=F32).astype(BF16)
+        ui = jnp.dot(bwd_ref[pl.ds(r1, tile), pl.ds(mine_k, nrow)], gst[...], preferred_element_type=F32).astype(BF16)
         for s in range(sources):
             both = jnp.concatenate([ur[:, s * cols : (s + 1) * cols], ui[:, s * cols : (s + 1) * cols]], axis=1)
             v = jnp.dot(both, colback_ref[...], preferred_element_type=F32)
@@ -366,14 +407,24 @@
     vm = pl.BlockSpec(memory_space=pltpu.VMEM)
     dma = pltpu.SemaphoreType.DMA
     block = (sources, strip, cols)
+    sum_d = (2, sources, nrow // 2, cols)
+    sum_h = (len(PAIRS), nrow // 2, cols)
     return pl.pallas_call(
         functools.partial(step_kernel, last),
-        out_shape=jax.ShapeDtypeStruct(block if last else (blocks,) + block, F32),
+        out_shape=jax.ShapeDtypeStruct(block, F32)
+        if last
+        else (
+            jax.ShapeDtypeStruct((blocks,) + block, F32),
+            jax.ShapeDtypeStruct(sum_d, BF16),
+            jax.ShapeDtypeStruct(sum_h, BF16),
+        ),
         in_specs=[vm] * 8 + [pl.BlockSpec(memory_space=pltpu.SMEM)],
-        out_specs=vm,
-        scratch_shapes=[
+        out_specs=vm if last else (vm, vm, vm),
+        scratch_shapes=([] if last else [pltpu.VMEM(sum_d, BF16), pltpu.VMEM(sum_h, BF16)])
+        + [
+            pltpu.VMEM((nrow, sources * cols), F32),
             pltpu.VMEM((2 * nrow, sources * cols), BF16),
-            pltpu.VMEM((2 * nrow, sources * cols), BF16),
+            pltpu.VMEM((nrow, sources * cols), BF16),
             pltpu.VMEM((4, 2, 2) + block, BF16),
             pltpu.VMEM((4, 2) + block, BF16),
             pltpu.VMEM((4, 2) + block, BF16),
@@ -385,7 +436,7 @@
             pltpu.VMEM((2, sources, 16, cols), BF16),
             dma((4,)), dma((4,)), dma((4,)), dma((4,)), dma((3,)), dma((3,)),
             dma((3,)), dma((3,)), dma((4,)), dma((4,)), dma((8,)), dma((8,)),
-            dma((2,)), dma((2,)),
+            dma((2,)), dma((2,)), dma((2,)), dma((2,)),
         ],
         compiler_params=pltpu.CompilerParams(
             collective_id=1 if last else 0, has_side_effects=True, vmem_limit_bytes=VMEM_LIMIT
@@ -393,35 +444,108 @@
     )(s_full, own, dd, hh, *tables, lam)
 
 
+def sums_kernel(d_ref, g_ref, mix_ref, level_ref, expand_ref, copy_d_ref, copy_h_ref, mask_d_ref, mask_h_ref,
+                dd_ref, hh_ref, wd_ref, wh_ref):
+    @pl.when(pl.program_id(0) == 0)
+    def _():
+        mix = mix_ref[...]
+        weighted = mix * (level_ref[...].astype(F32) * 0.25)
+        chans = mix.shape[1]
+        by_source = [jnp.broadcast_to(weighted[s : s + 1], (16, chans)) for s in range(4)]
+        by_pair = [jnp.broadcast_to(weighted[s : s + 1] * mix[t : t + 1], (8, chans)) for s, t in PAIRS]
+        wd = jnp.concatenate(by_source + by_source, axis=0).astype(BF16)
+        wh = jnp.concatenate(by_pair, axis=0).astype(BF16)
+        wd = jnp.dot(wd, copy_d_ref[...], preferred_element_type=F32) * mask_d_ref[...].astype(F32)
+        wh = jnp.dot(wh, copy_h_ref[...], preferred_element_type=F32) * mask_h_ref[...].astype(F32)
+        wd_ref[...] = wd.astype(BF16)
+        wh_ref[...] = wh.astype(BF16)
+
+    groups = g_ref.shape[0] // 8
+    chans, cols = g_ref.shape[1:]
+    wide = 4 * chans
+    half = cols // 2
+    for n in range(groups):
+        g = g_ref[8 * n : 8 * n + 8]
+        products = []
+        for j in range(0, 8, 2):
+            pair = [jnp.concatenate([g[k, :, :half], g[k, :, half:]], axis=0) for k in (j, j + 1)]
+            spread = jnp.dot(expand_ref[...], jnp.concatenate(pair, axis=1), preferred_element_type=F32)
+            for i in range(2):
+                row = (8 * n + j + i) * wide
+                d = d_ref[row : row + wide, :].astype(F32)
+                products.append((d * spread[:, i * half : (i + 1) * half]).astype(BF16))
+        total = jnp.dot(wd_ref[...], jnp.concatenate(products, axis=0), preferred_element_type=F32)
+        for z in range(2):
+            for s in range(4):
+                for lt in range(2):
+                    r = ((z * 4 + s) * 2 + lt) * 8
+                    dd_ref[z, s, 8 * n : 8 * n + 8, lt * half : (lt + 1) * half] = total[r : r + 8].astype(BF16)
+        squares = g.astype(F32)
+        squares = (squares * squares).astype(BF16).reshape(8 * chans, cols)
+        grams = jnp.dot(wh_ref[...], squares, preferred_element_type=F32)
+        for p in range(len(PAIRS)):
+            hh_ref[p, 8 * n : 8 * n + 8, :] = grams[8 * p : 8 * p + 8].astype(BF16)
+
+
 def channel_sums(sky_data, beam_gains, mixing, noise_levels):
-    weighted = mixing * (noise_levels.astype(F32) * 0.25)[:, None]
-    beam = beam_gains.astype(F32)
-    gd = (beam[:, :, None, :] * sky_data.astype(F32)).astype(BF16)
-    gg = (beam * beam).astype(BF16)
-    pair = jnp.stack([weighted[:, s] * mixing[:, t] for s, t in PAIRS], axis=1)
-    dd = jnp.einsum("cs,kczl->zskl", weighted.astype(BF16), gd, preferred_element_type=F32)
-    hh = jnp.einsum("cp,kcl->pkl", pair.astype(BF16), gg, preferred_element_type=F32)
-    return dd.astype(BF16), hh.astype(BF16)
+    nrow, chans, _, cols = sky_data.shape
+    half = cols // 2
+    ones = np.ones
+    eye = np.eye
+    mask_d = np.einsum("s,kK,lL,zZ,c->zslkKcLZ", ones(4), eye(8), eye(2), eye(2), ones(chans)).reshape(128, -1)
+    mask_h = np.einsum("p,kK,c->pkKc", ones(len(PAIRS)), eye(8), ones(chans)).reshape(8 * len(PAIRS), -1)
+    copy_d = np.einsum("cC,k,r->ckCr", eye(chans), ones(8), ones(4)).reshape(chans, -1)
+    copy_h = np.einsum("cC,k->ckC", eye(chans), ones(8)).reshape(chans, -1)
+    expand = np.einsum("cC,lL,z->clzLC", np.eye(chans), np.eye(2), np.ones(2)).reshape(4 * chans, 2 * chans)
+    rows = jnp.swapaxes(sky_data.reshape(nrow, chans, 2, 2, half), 2, 3).reshape(-1, half)
+    tile = 32
+    tables = [jnp.asarray(t.astype(ml_dtypes.bfloat16)) for t in (expand, copy_d, copy_h, mask_d, mask_h)]
+    return pl.pallas_call(
+        sums_kernel,
+        grid=(nrow // tile,),
+        out_shape=(
+            jax.ShapeDtypeStruct((2, 4, nrow, cols), BF16),
+            jax.ShapeDtypeStruct((len(PAIRS), nrow, cols), BF16),
+        ),
+        in_specs=[
+            pl.BlockSpec((tile * 4 * chans, half), lambda i: (i, 0)),
+            pl.BlockSpec((tile, chans, cols), lambda i: (i, 0, 0)),
+            pl.BlockSpec((4, chans), lambda i: (0, 0)),
+            pl.BlockSpec((1, chans), lambda i: (0, 0)),
+        ]
+        + [pl.BlockSpec(table.shape, lambda i: (0, 0)) for table in tables],
+        out_specs=(
+            pl.BlockSpec((2, 4, tile, cols), lambda i: (0, 0, i, 0)),
+            pl.BlockSpec((len(PAIRS), tile, cols), lambda i: (0, i, 0)),
+        ),
+        scratch_shapes=[pltpu.VMEM((128, 32 * chans), BF16), pltpu.VMEM((8 * len(PAIRS), 8 * chans), BF16)],
+        compiler_params=pltpu.CompilerParams(vmem_limit_bytes=VMEM_LIMIT),
+        cost_estimate=pl.CostEstimate(flops=2 * 10**9, bytes_accessed=30 * 10**6, transcendentals=0),
+    )(rows, beam_gains, mixing.T, noise_levels.reshape(1, chans), *tables)
 
 
 def body(sky_data, beam_gains, mixing, noise_levels, threshold_levels, start_sources):
     strip, sources, cols = start_sources.shape
     blocks = lax.axis_size("chan")
-    if blocks != 16 or strip != 32 or sources != 4 or cols % 128:
+    if blocks != 16 or strip != 32 or sources != 4 or cols != 256 or sky_data.shape[1] != 32:
         return plain_body(sky_data, beam_gains, mixing, noise_levels, threshold_levels, start_sources)
     row_real, row_imag = host_tables(strip * blocks)
     col_real, col_imag = host_tables(cols)
+    forward = np.block([[row_real, -row_imag], [row_imag, row_real]])
+    backward = np.block([[row_real, row_imag], [-row_imag, row_real]])
+    half_k = strip * blocks // 2
+    starts = [0, 2 * half_k, half_k, 3 * half_k]
     tables = [
         jnp.asarray(np.concatenate([col_real, col_imag], axis=1)),
         jnp.asarray(np.concatenate([col_real, col_imag], axis=0)),
-        jnp.asarray(np.block([[row_real, -row_imag], [row_imag, row_real]])),
-        jnp.asarray(np.block([[row_real, row_imag], [-row_imag, row_real]])),
+        jnp.asarray(np.concatenate([forward[part : part + half_k] for part in starts], axis=0)),
+        jnp.asarray(np.concatenate([backward[:, part : part + half_k] for part in starts], axis=1)),
     ]
     lam = threshold_levels.astype(F32) * 0.05
     own = jnp.swapaxes(start_sources, 0, 1)
     s_full = lax.all_gather(own.astype(BF16), "chan", axis=0)
     dd, hh = channel_sums(sky_data, beam_gains, mixing, noise_levels)
-    s_full = step(False, s_full, own, dd, hh, tables, lam)
+    s_full, dd, hh = step(False, s_full, own, dd, hh, tables, lam)
     result = step(True, s_full, own, dd, hh, tables, lam)
     return jnp.swapaxes(result, 0, 1)
 

time: 145 us -> 129 us (0.89)
  other arithmetic: 34.7 us -> 0.57 us
  Pallas kernels: 72.8 us -> 93.3 us
  waiting for transfers between devices: 0.02 us -> 15.7 us
  matrix products: 13.1 us -> 0 us
  local copies, waits for them, and re-layouts: 9.15 us -> 5.56 us
    convert_element_type x2 -> x0, other arithmetic: 34.1 us -> none  [the longest x1 22.8 us: channel_sums(): gd = (beam[:, :, None, :] * sky_data.astype(F32)).astype(BF16)]
    pallas_call x0 -> x1, Pallas kernels: none -> 23.4 us  [channel_sums(): pl.pallas_call(sums_kernel, grid=(nrow // tile,), out_shape=(jax.ShapeDty...]
    all_gather x1, waiting for transfers between devices: 0.01 us -> 15.7 us  [body(): s_full = lax.all_gather(own.astype(BF16), 'chan', axis=0)]
    dot_general x2 -> x0, matrix products: 13.1 us -> none  [the longest x1 8.13 us: channel_sums(): jnp.einsum('cs,kczl->zskl', weighted.astype(BF16), gd, preferred_element_...]
    dot_general x2 -> x0, local copies, waits for them, and re-layouts: 4.18 us -> none  [the longest x1 2.43 us: channel_sums(): jnp.einsum('cp,kcl->pkl', pair.astype(BF16), gg, preferred_element_type=F32)]
    pallas_call x2, Pallas kernels: 72.8 us -> 70 us  [step(): pl.pallas_call(functools.partial(step_kernel, last), out_shape=jax.ShapeD...]
    unnamed x9 -> x3, local copies, waits for them, and re-layouts: 3.26 us -> 3.91 us
  transfers between devices with their start and end apart: 1 -> 1, of which waited for: 0 -> 1; matrix products, arithmetic and copies ran while one was open for 38% -> 2% of each run, Pallas kernels for 0% -> 18%
where the time goes in v2:
time: 129 us
  Pallas kernels  93.3 us (72%)
  waiting for transfers between devices  15.7 us (12%)
  between operations  13.4 us (10%)
  local copies, waits for them, and re-layouts  5.56 us (4%)
    pallas_call x2, Pallas kernels, step(): pl.pallas_call(functools.partial(step_kernel, last), out_shape=jax.ShapeD...  70 us
    pallas_call x1, Pallas kernels, channel_sums(): pl.pallas_call(sums_kernel, grid=(nrow // tile,), out_shape=(jax.ShapeDty...  23.4 us
    all_gather x1, waiting for transfers between devices, body(): s_full = lax.all_gather(own.astype(BF16), 'chan', axis=0)  15.7 us
    unnamed x3, local copies, waits for them, and re-layouts  3.91 us
  transfers between devices with their start and end apart: 1, of which 1 were waited for; matrix products, arithmetic and copies ran while one was open for 2% of the time, Pallas kernels for 18%

profile of v2, /device:TPU:1, one launch (start us, length us, event | category | flops | bytes accessed | tf_op | source)
XLA Modules:
  0.0 128.5 jit_solution(3222150079217105351)
XLA Ops:
  6.5 0.0 all-gather.3.cloned.1.call-start
  6.5 1.6 %copy.28 = bf16[32,4,256]{2,0,1:T(8,128)(2,1)} copy(f32[32,4,256]{2,1,0:T(4,128)} %param.20) | data formatting | bytes 196608 | tf_op args[5]
  8.1 0.0 all-gather.3.cloned.1.call-update
  8.1 1.6 %copy.27 = f32[32,4,256]{2,0,1:T(8,128)} copy(f32[32,4,256]{2,1,0:T(4,128)} %param.20) | data formatting | bytes 262144 | tf_op args[5]
  9.7 0.8 copy.22
  10.5 23.4 %shard_map.145 = (bf16[2,4,512,256]{3,2,1,0:T(8,128)(2,1)}, bf16[10,512,256]{2,1,0:T(8,128)(2,1)}) custom-call(bf16[65536,128]{1,0:T(8,128)(2,1)} %bitcast.15, bf16[512,32,256]{2,1,0:T(8,128)(2,1)} %g_ref.1, f32[4,32]{1,0:T(4,128)} %bitcast.21, s32[1,32]{1,0:T(1,128)} %bitcast.22, bf16[128,64]{1,0:T(8,128)(2,1)} %constant.24.clone.expand_ref, ...), custom_call_target="tpu_custom_call" | custom-call | flops 2000000000 | bytes 30000000 | tf_op jit(solution)/shard_map/pallas_call | solution.py:503
  33.8 0.6 convert_multiply_fusion.lam_ref
  34.4 15.7 %all-gather.3.cloned.1.call-done = bf16[64,32,256]{2,1,0:T(8,128)(2,1)} async-done(((bf16[4,32,256]{2,1,0:T(8,128)(2,1)}), bf16[64,32,256]{2,1,0:T(8,128)(2,1)}) %all-gather.3.cloned.1.call-update) | async-done | bytes 1048592 | tf_op jit(solution)/shard_map/all_gather | solution.py:546
  50.1 44.2 %shard_map.146 = (f32[16,4,32,256]{3,2,1,0:T(8,128)}, bf16[2,4,256,256]{3,2,1,0:T(8,128)(2,1)}, bf16[10,256,256]{2,1,0:T(8,128)(2,1)}) custom-call(bf16[16,4,32,256]{3,2,1,0:T(8,128)(2,1)} %bitcast.18, f32[4,32,256]{2,1,0:T(8,128)} %bitcast.16, bf16[2,4,512,256]{3,2,1,0:T(8,128)(2,1)} %get-tuple-element.10.d_ref, ...), custom_call_target="tpu_custom_call" | custom-call | tf_op jit(solution)/shard_map/pallas_call | solution.py:412
  94.3 25.8 %shard_map.147 = f32[4,32,256]{2,1,0:T(8,128)} custom-call(f32[16,4,32,256]{3,2,1,0:T(8,128)} %get-tuple-element.12.s_ref, f32[4,32,256]{2,1,0:T(8,128)} %bitcast.17, bf16[2,4,256,256]{3,2,1,0:T(8,128)(2,1)} %get-tuple-element.13.d_ref, bf16[10,256,256]{2,1,0:T(8,128)(2,1)} %get-tuple-element.14.h_ref, bf16[256,512]{1,0:T(8,128)(2,1)} %constant.20.clone.colcat_ref, ...), custom_call_target="tpu_custom_call" | custom-call | tf_op jit(solution)/shard_map/pallas_call | solution.py:412
  120.1 1.6 %copy.23 = f32[32,4,256]{2,1,0:T(4,128)} copy(f32[32,4,256]{2,0,1:T(8,128)} %bitcast.19) | data formatting | bytes 262144 | tf_op jit(solution)/shard_map/transpose | solution.py:550
Async XLA Ops:
  6.5 43.5 %all-gather.3.cloned.1.call-start = ((), (), s32[]{:S(2)}) async-start(), calls=%async_computation | async-start | bytes 1114112 | tf_op jit(solution)/shard_map/all_gather | solution.py:546
Sparse Core Ops, SparseCore 0:
  9.5 40.4 all-gather.2

commit v3 on v0

--- a/solution.py
+++ b/solution.py
@@ -1,8 +1,13 @@
+import functools
 import math
 
 import jax
 import jax.numpy as jnp
+import ml_dtypes
+import numpy as np
 from jax import lax
+from jax.experimental import pallas as pl
+from jax.experimental.pallas import tpu as pltpu
 from jax.sharding import PartitionSpec as P
 
 ITERS = 2
@@ -108,7 +113,7 @@
     )
 
 
-def body(sky_data, beam_gains, mixing, noise_levels, threshold_levels, start_sources):
+def plain_body(sky_data, beam_gains, mixing, noise_levels, threshold_levels, start_sources):
     strip_rows, source_count, col_count = start_sources.shape
     full_rows = strip_rows * lax.axis_size("chan")
     row_real, row_imag = dft_tables(full_rows)
@@ -146,6 +151,427 @@
     return sources
 
 
+BF16 = jnp.bfloat16
+F32 = jnp.float32
+VMEM_LIMIT = 56 * 1024 * 1024
+PAIRS = [(s, t) for s in range(4) for t in range(s, 4)]
+PAIR_OF = {}
+for number, (first, second) in enumerate(PAIRS):
+    PAIR_OF[first, second] = number
+    PAIR_OF[second, first] = number
+
+
+def host_tables(length):
+    positions = np.arange(length)
+    angles = (positions[:, None] * positions[None, :] % length) * (2.0 * math.pi / length)
+    norm_factor = 1.0 / math.sqrt(length)
+    return (
+        (np.cos(angles) * norm_factor).astype(np.float32).astype(ml_dtypes.bfloat16),
+        (-np.sin(angles) * norm_factor).astype(np.float32).astype(ml_dtypes.bfloat16),
+    )
+
+
+def smooth_window(x, first_row, row_total, fine, coarse_bound):
+    height, width = x.shape
+    rows = lax.broadcasted_iota(jnp.int32, (height, width), 0) + first_row
+    lanes = lax.broadcasted_iota(jnp.int32, (height, width), 1)
+    inside = (rows >= 0) & (rows < row_total)
+
+    def smooth(v, d):
+        v = 0.25 * (pltpu.roll(v, d, 0) + 2.0 * v + pltpu.roll(v, height - d, 0))
+        left = jnp.where(lanes >= d, pltpu.roll(v, d, 1), 0.0)
+        right = jnp.where(lanes < width - d, pltpu.roll(v, width - d, 1), 0.0)
+        return 0.25 * (left + 2.0 * v + right)
+
+    c1 = jnp.where(inside, smooth(x, 1), 0.0)
+    c2 = smooth(c1, 2)
+    d1 = c1 - c2
+    d0 = x - c1
+    result = c2 + (d1 - jnp.clip(d1, -coarse_bound, coarse_bound)) + (d0 - jnp.clip(d0, -fine, fine))
+    return result[8 : height - 8]
+
+
+class Place:
+    def __init__(self):
+        self.me = me = lax.axis_index("chan")
+        self.z, self.y, self.c = z, y, c = me // 4, (me // 2) % 2, me % 2
+        self.core_peer = self.index(z, y, 1 - c)
+        self.y_peer = self.index(z, 1 - y, c)
+        self.z_peers = [self.index((z + 1 + i) % 4, y, c) for i in range(3)]
+        self.peers = [self.core_peer, self.y_peer] + self.z_peers
+
+    def index(self, z, y, c):
+        return z * 4 + y * 2 + c
+
+    def remote(self, src, dst, send, recv, peer):
+        return pltpu.make_async_remote_copy(
+            src_ref=src, dst_ref=dst, send_sem=send, recv_sem=recv,
+            device_id={"chan": peer}, device_id_type=pl.DeviceIdType.MESH,
+        )
+
+    def greet(self, peers):
+        barrier = pltpu.get_barrier_semaphore()
+        for peer in peers:
+            pl.semaphore_signal(barrier, inc=1, device_id={"chan": peer}, device_id_type=pl.DeviceIdType.MESH)
+
+    def gather(self, buf, gz_s, gz_r, gy_s, gy_r, gc_s, gc_r):
+        z, y, c = self.z, self.y, self.c
+        held = [self.index((z + 4 - j) % 4, y, c) for j in range(4)]
+        crossed = [self.index((z + 4 - j) % 4, 1 - y, c) for j in range(4)]
+
+        def send(block, s_sem, r_sem, peer):
+            return self.remote(buf.at[block], buf.at[block], s_sem, r_sem, peer)
+
+        gz = [send(held[0], gz_s.at[i], gz_r.at[i], self.z_peers[i]) for i in range(3)]
+        gy = [send(held[j], gy_s.at[j], gy_r.at[j], self.y_peer) for j in range(4)]
+        gc = [send(block, gc_s.at[j], gc_r.at[j], self.core_peer) for j, block in enumerate(held + crossed)]
+        return gz, gy, gc
+
+
+def steps_kernel(
+    s_ref, start_ref, d_ref, h_ref, colcat_ref, colback_ref, fwd_ref, bwd_ref, lam_ref, out_ref,
+    got_d, got_h, dsum_ref, hsum_ref, qst, pst, gst, vb, got_core, acc, got_y, fin, got_z, sall, own, xpad, halo,
+    core_s, core_r, y_s, y_r, z_s, z_r, gz_s, gz_r, gy_s, gy_r, gc_s, gc_r, halo_s, halo_r, half_s, half_r,
+):
+    blocks, sources, strip, cols = s_ref.shape
+    nrow = blocks * strip
+    place = Place()
+    me, z, y, c = place.me, place.z, place.y, place.c
+    remote = place.remote
+    right, left = (me + 1) % blocks, (me + blocks - 1) % blocks
+    greeted = place.peers + [left, right]
+    place.greet(greeted)
+    pl.semaphore_wait(pltpu.get_barrier_semaphore(), len(greeted))
+
+    half_k = nrow // 2
+    other = pl.ds(pl.multiple_of((1 - c) * half_k, half_k), half_k)
+    swap_d = remote(d_ref.at[:, :, other, :], got_d, half_s.at[0], half_r.at[0], place.core_peer)
+    swap_h = remote(h_ref.at[:, other, :], got_h, half_s.at[1], half_r.at[1], place.core_peer)
+    swap_d.start()
+    swap_h.start()
+    for s in range(sources):
+        own[s] = start_ref[:, s, :]
+
+    tile = 128
+    thin = 16
+    mine_k = pl.multiple_of(c * nrow, nrow)
+    for iteration in range(ITERS):
+        first, last = iteration == 0, iteration == ITERS - 1
+        now_ref = s_ref if first else sall
+
+        for t in range(sources):
+            p = jnp.dot(now_ref[:, t].reshape(nrow, cols), colcat_ref[...], preferred_element_type=F32)
+            pst[0:nrow, t * cols : (t + 1) * cols] = p[:, :cols].astype(BF16)
+            pst[nrow:, t * cols : (t + 1) * cols] = p[:, cols:].astype(BF16)
+
+        @pl.loop(0, nrow // tile)
+        def _(kb):
+            k0 = pl.multiple_of(kb * tile, tile)
+            rows = fwd_ref[pl.ds(pl.multiple_of(mine_k + k0, tile), tile), :]
+            qst[pl.ds(k0, tile), :] = jnp.dot(rows, pst[...], preferred_element_type=F32)
+
+        if first:
+            swap_d.wait()
+            swap_h.wait()
+
+        @pl.loop(0, half_k // thin)
+        def _(kb):
+            k0 = pl.multiple_of(kb * thin, thin)
+            here = pl.ds(k0, thin)
+            if first:
+                whole = pl.ds(pl.multiple_of(c * half_k + k0, thin), thin)
+                h = [(h_ref[p, whole, :].astype(F32) + got_h[p, here, :].astype(F32)) for p in range(len(PAIRS))]
+                for p in range(len(PAIRS)):
+                    hsum_ref[p, here, :] = h[p].astype(BF16)
+            else:
+                h = [hsum_ref[p, here, :].astype(F32) for p in range(len(PAIRS))]
+            for part in range(2):
+                rows = pl.ds(pl.multiple_of(part * half_k + k0, thin), thin)
+                q = [qst[rows, t * cols : (t + 1) * cols] for t in range(sources)]
+                for s in range(sources):
+                    if first:
+                        g = d_ref[part, s, whole, :].astype(F32) + got_d[part, s, here, :].astype(F32)
+                        dsum_ref[part, s, here, :] = g.astype(BF16)
+                    else:
+                        g = dsum_ref[part, s, here, :].astype(F32)
+                    for t in range(sources):
+                        g = g - h[PAIR_OF[s, t]] * q[t]
+                    gst[rows, s * cols : (s + 1) * cols] = g.astype(BF16)
+
+        core_copies, y_copies, z_copies = [], [], []
+
+        def do_core(i):
+            zb = (z + 1 + i) % 4
+            r0 = pl.multiple_of(zb * tile, tile)
+            r1 = pl.multiple_of(nrow + zb * tile, tile)
+            columns = pl.ds(mine_k, nrow)
+            ur = jnp.dot(bwd_ref[pl.ds(r0, tile), columns], gst[...], preferred_element_type=F32).astype(BF16)
+            ui = jnp.dot(bwd_ref[pl.ds(r1, tile), columns], gst[...], preferred_element_type=F32).astype(BF16)
+            for s in range(sources):
+                both = jnp.concatenate([ur[:, s * cols : (s + 1) * cols], ui[:, s * cols : (s + 1) * cols]], axis=1)
+                v = jnp.dot(both, colback_ref[...], preferred_element_type=F32)
+                vb[i, :, :, s] = v.astype(BF16).reshape(2, 2, strip, cols)
+            copy = remote(vb.at[i, :, 1 - c], got_core.at[i], core_s.at[i], core_r.at[i], place.core_peer)
+            copy.start()
+            core_copies.append(copy)
+
+        def do_y(i):
+            core_copies[i].wait()
+            acc[i] = (vb[i, :, c].astype(F32) + got_core[i].astype(F32)).astype(BF16)
+            copy = remote(acc.at[i, 1 - y], got_y.at[i], y_s.at[i], y_r.at[i], place.y_peer)
+            copy.start()
+            y_copies.append(copy)
+
+        def do_z(i):
+            y_copies[i].wait()
+            fin[i] = (acc[i, y].astype(F32) + got_y[i].astype(F32)).astype(BF16)
+            copy = remote(fin.at[i], got_z.at[i], z_s.at[i], z_r.at[i], place.z_peers[i])
+            copy.start()
+            z_copies.append(copy)
+
+        do_core(0)
+        do_core(1)
+        do_y(0)
+        do_core(2)
+        do_y(1)
+        do_z(0)
+        do_core(3)
+        do_y(2)
+        do_z(1)
+        do_y(3)
+        do_z(2)
+        y_copies[3].wait()
+        total = own[...] + (acc[3, y].astype(F32) + got_y[3].astype(F32))
+        for i in range(3):
+            z_copies[i].wait()
+            total = total + got_z[i].astype(F32)
+
+        xpad[:, 8 : 8 + strip] = total
+        to_right = remote(xpad.at[:, strip : strip + 8], halo.at[0], halo_s.at[0], halo_r.at[0], right)
+        to_left = remote(xpad.at[:, 8:16], halo.at[1], halo_s.at[1], halo_r.at[1], left)
+        to_right.start()
+        to_left.start()
+        to_right.wait()
+        to_left.wait()
+        xpad[:, 0:8] = jnp.where(me > 0, halo[0], 0.0)
+        xpad[:, 8 + strip : 16 + strip] = jnp.where(me < blocks - 1, halo[1], 0.0)
+        for s in range(sources):
+            result = smooth_window(xpad[s], me * strip - 8, nrow, lam_ref[s, 0], lam_ref[s, 1])
+            if last:
+                out_ref[:, s, :] = result
+            else:
+                own[s] = result
+                sall[me, s] = result.astype(BF16)
+
+        if not last:
+            gz, gy, gc = place.gather(sall, gz_s, gz_r, gy_s, gy_r, gc_s, gc_r)
+            for copy in gz + [gy[0], gc[0]]:
+                copy.start()
+            for j in range(1, 4):
+                gz[j - 1].wait_recv()
+                gy[j].start()
+                gc[j].start()
+            for j in range(4):
+                gy[j].wait_recv()
+                gc[4 + j].start()
+            for copy in gc:
+                copy.wait_recv()
+            for copy in gz + gy + gc:
+                copy.wait_send()
+
+
+def steps(s_full, start, dd, hh, tables, lam):
+    blocks, sources, strip, cols = s_full.shape
+    nrow = blocks * strip
+    vm = pl.BlockSpec(memory_space=pltpu.VMEM)
+    dma = pltpu.SemaphoreType.DMA
+    block = (sources, strip, cols)
+    sum_d = (2, sources, nrow // 2, cols)
+    sum_h = (len(PAIRS), nrow // 2, cols)
+    return pl.pallas_call(
+        steps_kernel,
+        out_shape=jax.ShapeDtypeStruct(start.shape, F32),
+        in_specs=[vm] * 8 + [pl.BlockSpec(memory_space=pltpu.SMEM)],
+        out_specs=vm,
+        scratch_shapes=[
+            pltpu.VMEM(sum_d, BF16),
+            pltpu.VMEM(sum_h, BF16),
+            pltpu.VMEM(sum_d, BF16),
+            pltpu.VMEM(sum_h, BF16),
+            pltpu.VMEM((nrow, sources * cols), F32),
+            pltpu.VMEM((2 * nrow, sources * cols), BF16),
+            pltpu.VMEM((nrow, sources * cols), BF16),
+            pltpu.VMEM((4, 2, 2) + block, BF16),
+            pltpu.VMEM((4, 2) + block, BF16),
+            pltpu.VMEM((4, 2) + block, BF16),
+            pltpu.VMEM((4,) + block, BF16),
+            pltpu.VMEM((3,) + block, BF16),
+            pltpu.VMEM((3,) + block, BF16),
+            pltpu.VMEM((blocks,) + block, BF16),
+            pltpu.VMEM(block, F32),
+            pltpu.VMEM((sources, strip + 16, cols), F32),
+            pltpu.VMEM((2, sources, 8, cols), F32),
+            dma((4,)), dma((4,)), dma((4,)), dma((4,)), dma((3,)), dma((3,)),
+            dma((3,)), dma((3,)), dma((4,)), dma((4,)), dma((8,)), dma((8,)),
+            dma((2,)), dma((2,)), dma((2,)), dma((2,)),
+        ],
+        compiler_params=pltpu.CompilerParams(collective_id=0, has_side_effects=True, vmem_limit_bytes=VMEM_LIMIT),
+    )(s_full, start, dd, hh, *tables, lam)
+
+
+def sums_kernel(start_ref, d_ref, g_ref, mix_ref, level_ref, expand_ref, copy_d_ref, copy_h_ref, mask_d_ref, mask_h_ref,
+                dd_ref, hh_ref, s_ref, wd_ref, wh_ref, own, own_sem, *gather_sems):
+    at = pl.program_id(0)
+    place = Place()
+    gz, gy, gc = place.gather(s_ref, *gather_sems)
+    keep = pltpu.make_async_copy(own, s_ref.at[place.me], own_sem)
+
+    @pl.when(at == 0)
+    def _():
+        place.greet(place.peers)
+        for s in range(4):
+            own[s] = start_ref[:, s, :].astype(BF16)
+        keep.start()
+
+    @pl.when(at == 1)
+    def _():
+        keep.wait()
+        pl.semaphore_wait(pltpu.get_barrier_semaphore(), len(place.peers))
+        for copy in gz + [gy[0], gc[0]]:
+            copy.start()
+
+    @pl.when(at == 5)
+    def _():
+        for j in range(1, 4):
+            gz[j - 1].wait_recv()
+            gy[j].start()
+            gc[j].start()
+
+    @pl.when(at == 9)
+    def _():
+        for j in range(4):
+            gy[j].wait_recv()
+            gc[4 + j].start()
+
+    @pl.when(at == pl.num_programs(0) - 1)
+    def _():
+        for copy in gc:
+            copy.wait_recv()
+        for copy in gz + gy + gc:
+            copy.wait_send()
+
+    @pl.when(pl.program_id(0) == 0)
+    def _():
+        mix = mix_ref[...]
+        weighted = mix * (level_ref[...].astype(F32) * 0.25)
+        chans = mix.shape[1]
+        by_source = [jnp.broadcast_to(weighted[s : s + 1], (16, chans)) for s in range(4)]
+        by_pair = [jnp.broadcast_to(weighted[s : s + 1] * mix[t : t + 1], (8, chans)) for s, t in PAIRS]
+        wd = jnp.concatenate(by_source + by_source, axis=0).astype(BF16)
+        wh = jnp.concatenate(by_pair, axis=0).astype(BF16)
+        wd = jnp.dot(wd, copy_d_ref[...], preferred_element_type=F32) * mask_d_ref[...].astype(F32)
+        wh = jnp.dot(wh, copy_h_ref[...], preferred_element_type=F32) * mask_h_ref[...].astype(F32)
+        wd_ref[...] = wd.astype(BF16)
+        wh_ref[...] = wh.astype(BF16)
+
+    groups = g_ref.shape[0] // 16
+    chans, cols = g_ref.shape[1:]
+    wide = 4 * chans
+    half = cols // 2
+    for n in range(groups):
+        products = []
+        for j in range(8):
+            ks = (16 * n + j, 16 * n + 8 + j)
+            pair = [jnp.concatenate([g_ref[k, :, :half], g_ref[k, :, half:]], axis=0) for k in ks]
+            spread = jnp.dot(expand_ref[...], jnp.concatenate(pair, axis=1), preferred_element_type=F32)
+            d = jnp.concatenate([d_ref[k * wide : (k + 1) * wide, :] for k in ks], axis=1)
+            products.append((d.astype(F32) * spread).astype(BF16))
+        total = jnp.dot(wd_ref[...], jnp.concatenate(products, axis=0), preferred_element_type=F32)
+        for r in range(16):
+            z, s, lt = r // 8, r // 2 % 4, r % 2
+            rows = total[8 * r : 8 * r + 8]
+            both = jnp.concatenate([rows[:, :half], rows[:, half:]], axis=0)
+            dd_ref[z, s, 16 * n : 16 * n + 16, lt * half : (lt + 1) * half] = both.astype(BF16)
+        grams = []
+        for k in (16 * n, 16 * n + 8):
+            squares = g_ref[k : k + 8].astype(F32)
+            squares = (squares * squares).astype(BF16).reshape(8 * chans, cols)
+            grams.append(jnp.dot(wh_ref[...], squares, preferred_element_type=F32))
+        for p in range(len(PAIRS)):
+            both = jnp.concatenate([gram[8 * p : 8 * p + 8] for gram in grams], axis=0)
+            hh_ref[p, 16 * n : 16 * n + 16, :] = both.astype(BF16)
+
+
+def channel_sums(sky_data, beam_gains, mixing, noise_levels, start):
+    nrow, chans, _, cols = sky_data.shape
+    strip, sources, _ = start.shape
+    blocks = nrow // strip
+    dma = pltpu.SemaphoreType.DMA
+    half = cols // 2
+    ones = np.ones
+    eye = np.eye
+    mask_d = np.einsum("s,kK,lL,zZ,c->zslkKcLZ", ones(4), eye(8), eye(2), eye(2), ones(chans)).reshape(128, -1)
+    mask_h = np.einsum("p,kK,c->pkKc", ones(len(PAIRS)), eye(8), ones(chans)).reshape(8 * len(PAIRS), -1)
+    copy_d = np.einsum("cC,k,r->ckCr", eye(chans), ones(8), ones(4)).reshape(chans, -1)
+    copy_h = np.einsum("cC,k->ckC", eye(chans), ones(8)).reshape(chans, -1)
+    expand = np.einsum("cC,lL,z->clzLC", np.eye(chans), np.eye(2), np.ones(2)).reshape(4 * chans, 2 * chans)
+    rows = jnp.swapaxes(sky_data.reshape(nrow, chans, 2, 2, half), 2, 3).reshape(-1, half)
+    tile = 32
+    tables = [jnp.asarray(t.astype(ml_dtypes.bfloat16)) for t in (expand, copy_d, copy_h, mask_d, mask_h)]
+    return pl.pallas_call(
+        sums_kernel,
+        grid=(nrow // tile,),
+        out_shape=(
+            jax.ShapeDtypeStruct((2, 4, nrow, cols), BF16),
+            jax.ShapeDtypeStruct((len(PAIRS), nrow, cols), BF16),
+            jax.ShapeDtypeStruct((blocks, sources, strip, cols), BF16),
+        ),
+        in_specs=[
+            pl.BlockSpec(start.shape, lambda i: (0, 0, 0)),
+            pl.BlockSpec((tile * 4 * chans, half), lambda i: (i, 0)),
+            pl.BlockSpec((tile, chans, cols), lambda i: (i, 0, 0)),
+            pl.BlockSpec((4, chans), lambda i: (0, 0)),
+            pl.BlockSpec((1, chans), lambda i: (0, 0)),
+        ]
+        + [pl.BlockSpec(table.shape, lambda i: (0, 0)) for table in tables],
+        out_specs=(
+            pl.BlockSpec((2, 4, tile, cols), lambda i: (0, 0, i, 0)),
+            pl.BlockSpec((len(PAIRS), tile, cols), lambda i: (0, i, 0)),
+            pl.BlockSpec(memory_space=pl.ANY),
+        ),
+        scratch_shapes=[
+            pltpu.VMEM((128, 32 * chans), BF16),
+            pltpu.VMEM((8 * len(PAIRS), 8 * chans), BF16),
+            pltpu.VMEM((sources, strip, cols), BF16),
+            dma, dma((3,)), dma((3,)), dma((4,)), dma((4,)), dma((8,)), dma((8,)),
+        ],
+        compiler_params=pltpu.CompilerParams(collective_id=1, has_side_effects=True, vmem_limit_bytes=VMEM_LIMIT),
+        cost_estimate=pl.CostEstimate(flops=2 * 10**9, bytes_accessed=30 * 10**6, transcendentals=0),
+    )(start, rows, beam_gains, mixing.T, noise_levels.reshape(1, chans), *tables)
+
+
+def body(sky_data, beam_gains, mixing, noise_levels, threshold_levels, start_sources):
+    strip, sources, cols = start_sources.shape
+    blocks = lax.axis_size("chan")
+    if blocks != 16 or strip != 32 or sources != 4 or cols != 256 or sky_data.shape[1] != 32:
+        return plain_body(sky_data, beam_gains, mixing, noise_levels, threshold_levels, start_sources)
+    row_real, row_imag = host_tables(strip * blocks)
+    col_real, col_imag = host_tables(cols)
+    forward = np.block([[row_real, -row_imag], [row_imag, row_real]])
+    backward = np.block([[row_real, row_imag], [-row_imag, row_real]])
+    half_k = strip * blocks // 2
+    starts = [0, 2 * half_k, half_k, 3 * half_k]
+    tables = [
+        jnp.asarray(np.concatenate([col_real, col_imag], axis=1)),
+        jnp.asarray(np.concatenate([col_real, col_imag], axis=0)),
+        jnp.asarray(np.concatenate([forward[part : part + half_k] for part in starts], axis=0)),
+        jnp.asarray(np.concatenate([backward[:, part : part + half_k] for part in starts], axis=1)),
+    ]
+    lam = threshold_levels.astype(F32) * 0.05
+    dd, hh, s_full = channel_sums(sky_data, beam_gains, mixing, noise_levels, start_sources)
+    return steps(s_full, start_sources, dd, hh, tables, lam)
+
+
 def solution(mesh):
     return jax.shard_map(
         body,

time: 391 us -> 91 us (0.23); the launches traced: 385 us -> 90.2 us
  waiting for transfers between devices: 186 us -> 0 us
  matrix products: 104 us -> 0 us
  Pallas kernels: 0 us -> 87.3 us
  other arithmetic: 33.6 us -> 0.58 us
  local copies, waits for them, and re-layouts: 24.9 us -> 2.33 us
  starting transfers between devices: 22.4 us -> 0 us
  between operations: 13.8 us -> 0.02 us
    reduce_scatter x2 -> x0, waiting for transfers between devices: 117 us -> none  [body(): lax.psum_scatter(inverse_rows(row_real, row_imag, packed_grad, col_back,...]
    dot_general x14 -> x0, matrix products: 104 us -> none  [the longest x2 48.1 us: block_gradient(): summed = jnp.einsum('cs,kczl->kszl', mix_block, weighted)]
    pallas_call x0 -> x2, Pallas kernels: none -> 87.3 us  [the longest x1 62.9 us: steps(): pl.pallas_call(steps_kernel, out_shape=jax.ShapeDtypeStruct(start.shape,...]
    all_gather x2 -> x0, waiting for transfers between devices: 55.7 us -> none  [body(): gathered = lax.all_gather(rounded, 'chan', axis=0, tiled=True)]
    ppermute x8 -> x0, starting transfers between devices: 22.2 us -> none  [the longest x4 13.6 us: padded_2(): lax.ppermute(tail, axis, [(i, (i + 1) % count) for i in range(ends)])]
    convert_element_type x4 -> x0, other arithmetic: 14.8 us -> none  [the longest x1 11.3 us: block_gradient(): beam_gain = beam_block.astype(jnp.float32)[:, :, None, :]]
    ppermute x8 -> x0, waiting for transfers between devices: 12.9 us -> none  [the longest x4 12.9 us: padded_2(): lax.ppermute(head, axis, [((i + 1) % count, i) for i in range(ends)])]
    mul x9 -> x1, other arithmetic: 12.2 us -> 0.58 us  [body(): lam = threshold_levels.astype(F32) * 0.05]
  transfers between devices with their start and end apart: 12 -> 0, of which waited for: 8 -> 0; matrix products, arithmetic and copies ran while one was open for 6% -> 0% of each run, Pallas kernels for 0% -> 0%
where the time goes in v3:
time: 91 us; the launch traced here: 90.2 us
  Pallas kernels  87.3 us (96%)
  local copies, waits for them, and re-layouts  2.33 us (3%)
    pallas_call x1, Pallas kernels, steps(): pl.pallas_call(steps_kernel, out_shape=jax.ShapeDtypeStruct(start.shape,...  62.9 us
    pallas_call x1, Pallas kernels, channel_sums(): pl.pallas_call(sums_kernel, grid=(nrow // tile,), out_shape=(jax.ShapeDty...  24.4 us
    unnamed x2, local copies, waits for them, and re-layouts  2.33 us

profile of v3, /device:TPU:1, one launch (start us, length us, event | category | flops | bytes accessed | tf_op | source)
XLA Modules:
  0.0 90.2 jit_solution(1227832105597802444)
XLA Ops:
  0.0 0.8 copy.17
  0.8 0.6 convert_multiply_fusion.lam_ref
  1.3 24.4 %shard_map.145 = (bf16[2,4,512,256]{3,2,1,0:T(8,128)(2,1)}, bf16[10,512,256]{2,1,0:T(8,128)(2,1)}, bf16[16,4,32,256]{3,2,1,0:T(8,128)(2,1)}) custom-call(f32[32,4,256]{2,1,0:T(4,128)} %start_ref.3, bf16[65536,128]{1,0:T(8,128)(2,1)} %bitcast.7, bf16[512,32,256]{2,1,0:T(8,128)(2,1)} %g_ref.1, f32[4,32]{1,0:T(4,128)} %bitcast.8, s32[1,32]{1,0:T(1,128)} %bitcast.9, ...), custom_call_target="tpu_custom_call" | custom-call | flops 2000000000 | bytes 30000000 | tf_op jit(solution)/shard_map/pallas_call | solution.py:521
  25.8 62.9 %shard_map.146 = f32[32,4,256]{2,1,0:T(4,128)} custom-call(bf16[16,4,32,256]{3,2,1,0:T(8,128)(2,1)} %get-tuple-element.8.s_ref, f32[32,4,256]{2,1,0:T(4,128)} %start_ref.3, bf16[2,4,512,256]{3,2,1,0:T(8,128)(2,1)} %get-tuple-element.9.d_ref, bf16[10,512,256]{2,1,0:T(8,128)(2,1)} %get-tuple-element.10.h_ref, bf16[256,512]{1,0:T(8,128)(2,1)} %constant.20.clone.colcat_ref, ...), custom_call_target="tpu_custom_call" | custom-call | tf_op jit(solution)/shard_map/pallas_call | solution.py:391
  88.7 1.6 %copy.19 = f32[32,4,256]{2,1,0:T(4,128)} copy(f32[32,4,256]{2,1,0:T(4,128)} %shard_map.146) | data formatting | bytes 262144

commit v4 on v3

--- a/solution.py
+++ b/solution.py
@@ -229,8 +229,8 @@
 
 
 def steps_kernel(
-    s_ref, start_ref, d_ref, h_ref, colcat_ref, colback_ref, fwd_ref, bwd_ref, lam_ref, out_ref,
-    got_d, got_h, dsum_ref, hsum_ref, qst, pst, gst, vb, got_core, acc, got_y, fin, got_z, sall, own, xpad, halo,
+    s_ref, start_ref, d_ref, h_ref, colcat_ref, colback_ref, fwd_ref, bwd_ref, level_ref, out_ref,
+    fwd_half, bwd_half, load, got_d, got_h, dsum_ref, hsum_ref, qst, pst, gst, vb, got_core, acc, got_y, fin, got_z, sall, own, xpad, halo,
     core_s, core_r, y_s, y_r, z_s, z_r, gz_s, gz_r, gy_s, gy_r, gc_s, gc_r, halo_s, halo_r, half_s, half_r,
 ):
     blocks, sources, strip, cols = s_ref.shape
@@ -241,9 +241,18 @@
     right, left = (me + 1) % blocks, (me + blocks - 1) % blocks
     greeted = place.peers + [left, right]
     place.greet(greeted)
+
+    half_k = nrow // 2
+    mine_k = pl.multiple_of(c * nrow, nrow)
+    keep_k = pl.ds(pl.multiple_of(c * half_k, half_k), half_k)
+    load_fwd = pltpu.make_async_copy(fwd_ref.at[pl.ds(mine_k, nrow), :], fwd_half, load.at[0])
+    load_h = pltpu.make_async_copy(h_ref.at[:, keep_k, :], hsum_ref, load.at[1])
+    load_d = pltpu.make_async_copy(d_ref.at[:, :, keep_k, :], dsum_ref, load.at[2])
+    load_bwd = pltpu.make_async_copy(bwd_ref.at[:, pl.ds(mine_k, nrow)], bwd_half, load.at[3])
+    for copy in (load_fwd, load_h, load_d, load_bwd):
+        copy.start()
     pl.semaphore_wait(pltpu.get_barrier_semaphore(), len(greeted))
 
-    half_k = nrow // 2
     other = pl.ds(pl.multiple_of((1 - c) * half_k, half_k), half_k)
     swap_d = remote(d_ref.at[:, :, other, :], got_d, half_s.at[0], half_r.at[0], place.core_peer)
     swap_h = remote(h_ref.at[:, other, :], got_h, half_s.at[1], half_r.at[1], place.core_peer)
@@ -252,9 +261,11 @@
     for s in range(sources):
         own[s] = start_ref[:, s, :]
 
+    def bound(s, j):
+        return level_ref[s, j].astype(F32) * 0.05
+
     tile = 128
     thin = 16
-    mine_k = pl.multiple_of(c * nrow, nrow)
     for iteration in range(ITERS):
         first, last = iteration == 0, iteration == ITERS - 1
         now_ref = s_ref if first else sall
@@ -264,13 +275,14 @@
             pst[0:nrow, t * cols : (t + 1) * cols] = p[:, :cols].astype(BF16)
             pst[nrow:, t * cols : (t + 1) * cols] = p[:, cols:].astype(BF16)
 
-        @pl.loop(0, nrow // tile)
-        def _(kb):
-            k0 = pl.multiple_of(kb * tile, tile)
-            rows = fwd_ref[pl.ds(pl.multiple_of(mine_k + k0, tile), tile), :]
-            qst[pl.ds(k0, tile), :] = jnp.dot(rows, pst[...], preferred_element_type=F32)
+            if first and t == 0:
+                load_fwd.wait()
+            block = slice(t * cols, (t + 1) * cols)
+            qst[:, block] = jnp.dot(fwd_half[...], pst[:, block], preferred_element_type=F32)
 
         if first:
+            load_h.wait()
+            load_d.wait()
             swap_d.wait()
             swap_h.wait()
 
@@ -279,8 +291,7 @@
             k0 = pl.multiple_of(kb * thin, thin)
             here = pl.ds(k0, thin)
             if first:
-                whole = pl.ds(pl.multiple_of(c * half_k + k0, thin), thin)
-                h = [(h_ref[p, whole, :].astype(F32) + got_h[p, here, :].astype(F32)) for p in range(len(PAIRS))]
+                h = [(hsum_ref[p, here, :].astype(F32) + got_h[p, here, :].astype(F32)) for p in range(len(PAIRS))]
                 for p in range(len(PAIRS)):
                     hsum_ref[p, here, :] = h[p].astype(BF16)
             else:
@@ -290,7 +301,7 @@
                 q = [qst[rows, t * cols : (t + 1) * cols] for t in range(sources)]
                 for s in range(sources):
                     if first:
-                        g = d_ref[part, s, whole, :].astype(F32) + got_d[part, s, here, :].astype(F32)
+                        g = dsum_ref[part, s, here, :].astype(F32) + got_d[part, s, here, :].astype(F32)
                         dsum_ref[part, s, here, :] = g.astype(BF16)
                     else:
                         g = dsum_ref[part, s, here, :].astype(F32)
@@ -302,15 +313,13 @@
 
         def do_core(i):
             zb = (z + 1 + i) % 4
-            r0 = pl.multiple_of(zb * tile, tile)
-            r1 = pl.multiple_of(nrow + zb * tile, tile)
-            columns = pl.ds(mine_k, nrow)
-            ur = jnp.dot(bwd_ref[pl.ds(r0, tile), columns], gst[...], preferred_element_type=F32).astype(BF16)
-            ui = jnp.dot(bwd_ref[pl.ds(r1, tile), columns], gst[...], preferred_element_type=F32).astype(BF16)
+            rows = pl.ds(pl.multiple_of(2 * zb * tile, 2 * tile), 2 * tile)
+            u = jnp.dot(bwd_half[rows, :], gst[...], preferred_element_type=F32).astype(BF16)
+            both = [u[:, s * cols : (s + 1) * cols] for s in range(sources)]
+            both = [jnp.concatenate([part[:tile], part[tile:]], axis=1) for part in both]
+            v = jnp.dot(jnp.concatenate(both, axis=0), colback_ref[...], preferred_element_type=F32).astype(BF16)
             for s in range(sources):
-                both = jnp.concatenate([ur[:, s * cols : (s + 1) * cols], ui[:, s * cols : (s + 1) * cols]], axis=1)
-                v = jnp.dot(both, colback_ref[...], preferred_element_type=F32)
-                vb[i, :, :, s] = v.astype(BF16).reshape(2, 2, strip, cols)
+                vb[i, :, :, s] = v[s * tile : (s + 1) * tile].reshape(2, 2, strip, cols)
             copy = remote(vb.at[i, :, 1 - c], got_core.at[i], core_s.at[i], core_r.at[i], place.core_peer)
             copy.start()
             core_copies.append(copy)
@@ -329,6 +338,8 @@
             copy.start()
             z_copies.append(copy)
 
+        if first:
+            load_bwd.wait()
         do_core(0)
         do_core(1)
         do_y(0)
@@ -356,7 +367,7 @@
         xpad[:, 0:8] = jnp.where(me > 0, halo[0], 0.0)
         xpad[:, 8 + strip : 16 + strip] = jnp.where(me < blocks - 1, halo[1], 0.0)
         for s in range(sources):
-            result = smooth_window(xpad[s], me * strip - 8, nrow, lam_ref[s, 0], lam_ref[s, 1])
+            result = smooth_window(xpad[s], me * strip - 8, nrow, bound(s, 0), bound(s, 1))
             if last:
                 out_ref[:, s, :] = result
             else:
@@ -380,10 +391,10 @@
                 copy.wait_send()
 
 
-def steps(s_full, start, dd, hh, tables, lam):
+def steps(s_full, start, dd, hh, tables, levels):
     blocks, sources, strip, cols = s_full.shape
     nrow = blocks * strip
-    vm = pl.BlockSpec(memory_space=pltpu.VMEM)
+    vm, hbm = pl.BlockSpec(memory_space=pltpu.VMEM), pl.BlockSpec(memory_space=pl.ANY)
     dma = pltpu.SemaphoreType.DMA
     block = (sources, strip, cols)
     sum_d = (2, sources, nrow // 2, cols)
@@ -391,9 +402,12 @@
     return pl.pallas_call(
         steps_kernel,
         out_shape=jax.ShapeDtypeStruct(start.shape, F32),
-        in_specs=[vm] * 8 + [pl.BlockSpec(memory_space=pltpu.SMEM)],
+        in_specs=[vm] * 2 + [hbm] * 2 + [vm] * 2 + [hbm] * 2 + [pl.BlockSpec(memory_space=pltpu.SMEM)],
         out_specs=vm,
         scratch_shapes=[
+            pltpu.VMEM((nrow, 2 * nrow), BF16),
+            pltpu.VMEM((2 * nrow, nrow), BF16),
+            dma((4,)),
             pltpu.VMEM(sum_d, BF16),
             pltpu.VMEM(sum_h, BF16),
             pltpu.VMEM(sum_d, BF16),
@@ -416,7 +430,7 @@
             dma((2,)), dma((2,)), dma((2,)), dma((2,)),
         ],
         compiler_params=pltpu.CompilerParams(collective_id=0, has_side_effects=True, vmem_limit_bytes=VMEM_LIMIT),
-    )(s_full, start, dd, hh, *tables, lam)
+    )(s_full, start, dd, hh, *tables, levels)
 
 
 def sums_kernel(start_ref, d_ref, g_ref, mix_ref, level_ref, expand_ref, copy_d_ref, copy_h_ref, mask_d_ref, mask_h_ref,
@@ -485,7 +499,7 @@
             pair = [jnp.concatenate([g_ref[k, :, :half], g_ref[k, :, half:]], axis=0) for k in ks]
             spread = jnp.dot(expand_ref[...], jnp.concatenate(pair, axis=1), preferred_element_type=F32)
             d = jnp.concatenate([d_ref[k * wide : (k + 1) * wide, :] for k in ks], axis=1)
-            products.append((d.astype(F32) * spread).astype(BF16))
+            products.append(d * spread.astype(BF16))
         total = jnp.dot(wd_ref[...], jnp.concatenate(products, axis=0), preferred_element_type=F32)
         for r in range(16):
             z, s, lt = r // 8, r // 2 % 4, r % 2
@@ -494,8 +508,7 @@
             dd_ref[z, s, 16 * n : 16 * n + 16, lt * half : (lt + 1) * half] = both.astype(BF16)
         grams = []
         for k in (16 * n, 16 * n + 8):
-            squares = g_ref[k : k + 8].astype(F32)
-            squares = (squares * squares).astype(BF16).reshape(8 * chans, cols)
+            squares = (g_ref[k : k + 8] * g_ref[k : k + 8]).reshape(8 * chans, cols)
             grams.append(jnp.dot(wh_ref[...], squares, preferred_element_type=F32))
         for p in range(len(PAIRS)):
             both = jnp.concatenate([gram[8 * p : 8 * p + 8] for gram in grams], axis=0)
@@ -559,6 +572,8 @@
     col_real, col_imag = host_tables(cols)
     forward = np.block([[row_real, -row_imag], [row_imag, row_real]])
     backward = np.block([[row_real, row_imag], [-row_imag, row_real]])
+    quarter = strip * blocks // 4
+    backward = backward.reshape(2, 4, quarter, -1).swapaxes(0, 1).reshape(8 * quarter, -1)
     half_k = strip * blocks // 2
     starts = [0, 2 * half_k, half_k, 3 * half_k]
     tables = [
@@ -567,9 +582,8 @@
         jnp.asarray(np.concatenate([forward[part : part + half_k] for part in starts], axis=0)),
         jnp.asarray(np.concatenate([backward[:, part : part + half_k] for part in starts], axis=1)),
     ]
-    lam = threshold_levels.astype(F32) * 0.05
     dd, hh, s_full = channel_sums(sky_data, beam_gains, mixing, noise_levels, start_sources)
-    return steps(s_full, start_sources, dd, hh, tables, lam)
+    return steps(s_full, start_sources, dd, hh, tables, threshold_levels)
 
 
 def solution(mesh):

time: 91 us -> 88.9 us (0.977)
  Pallas kernels: 87.3 us -> 85 us
    pallas_call x1, Pallas kernels: 62.9 us -> 60.6 us  [steps(): pl.pallas_call(steps_kernel, out_shape=jax.ShapeDtypeStruct(start.shape,...]
where the time goes in v4:
time: 88.9 us; the launch traced here: 87.9 us
  Pallas kernels  85 us (96%)
  local copies, waits for them, and re-layouts  2.9 us (3%)
    pallas_call x1, Pallas kernels, steps(): pl.pallas_call(steps_kernel, out_shape=jax.ShapeDtypeStruct(start.shape,...  60.6 us
    pallas_call x1, Pallas kernels, channel_sums(): pl.pallas_call(sums_kernel, grid=(nrow // tile,), out_shape=(jax.ShapeDty...  24.4 us
    unnamed x2, local copies, waits for them, and re-layouts  2.9 us

profile of v4, /device:TPU:1, one launch (start us, length us, event | category | flops | bytes accessed | tf_op | source)
XLA Modules:
  0.0 87.9 jit_solution(18410238601367263068)
XLA Ops:
  0.0 1.3 %copy.17.level_ref = s32[4,2]{1,0:T(4,128)} copy(s32[4,2]{0,1:T(2,128)} %param.19) | data formatting | bytes 64 | tf_op args[4]
  1.3 24.4 %shard_map.145 = (bf16[2,4,512,256]{3,2,1,0:T(8,128)(2,1)}, bf16[10,512,256]{2,1,0:T(8,128)(2,1)}, bf16[16,4,32,256]{3,2,1,0:T(8,128)(2,1)}) custom-call(f32[32,4,256]{2,1,0:T(4,128)} %start_ref.3, bf16[65536,128]{1,0:T(8,128)(2,1)} %bitcast.7, bf16[512,32,256]{2,1,0:T(8,128)(2,1)} %g_ref.1, f32[4,32]{1,0:T(4,128)} %bitcast.8, s32[1,32]{1,0:T(1,128)} %bitcast.9, ...), custom_call_target="tpu_custom_call" | custom-call | flops 2000000000 | bytes 30000000 | tf_op jit(solution)/shard_map/pallas_call | solution.py:534
  25.8 60.6 %shard_map.146 = f32[32,4,256]{2,1,0:T(4,128)} custom-call(bf16[16,4,32,256]{3,2,1,0:T(8,128)(2,1)} %get-tuple-element.8.s_ref, f32[32,4,256]{2,1,0:T(4,128)} %start_ref.3, bf16[2,4,512,256]{3,2,1,0:T(8,128)(2,1)} %get-tuple-element.9.d_ref, bf16[10,512,256]{2,1,0:T(8,128)(2,1)} %get-tuple-element.10.h_ref, bf16[256,512]{1,0:T(8,128)(2,1)} %constant.18.clone.colcat_ref, ...), custom_call_target="tpu_custom_call" | custom-call | tf_op jit(solution)/shard_map/pallas_call | solution.py:402
  86.4 1.6 %copy.19 = f32[32,4,256]{2,1,0:T(4,128)} copy(f32[32,4,256]{2,1,0:T(4,128)} %shard_map.146) | data formatting | bytes 262144
